TPU v7x, 256 devices: a whole 4x4x8 slice. The times are simulated.
256 devices in a mesh: band: 32 (over x_hi, z, core), pencil: 8 (over x_lo, y).
Axes of the slice: x: 4 (x_hi: 2, x_lo: 2; x = x_hi * 2 + x_lo), y: 4, z: 8, core: 2. Of those that a mesh axis runs over, the one named last changes fastest.
Arguments:
- orbitals: float32 [64, 72, 5184], P('band', 'pencil'), may hold values from -6 to 6
- pair_mask: int32 [32, 2, 2, 2], P('band'), may hold values 0 or 1
Outputs:
- exchange_term: float32 [64, 72, 5184], P('band', 'pencil')
All inputs are finite; a program needn't handle non-finite values. No bound on the sum of `pair_mask` on one device may be relied on, other than what follows from the above.
Results may differ from a plain program's by a relative error of at most 0.0001.
Values sent between devices are 32-bit elements; how exact they have to be, the bound alone decides.
A program may use at most 64 MiB of HBM per device.

v0:
```python
import functools
import math

import jax
import jax.numpy as jnp
import ml_dtypes
import numpy as np
from jax import lax
from jax.experimental import pallas as pl
from jax.experimental.pallas import tpu as pltpu
from jax.sharding import PartitionSpec as P

MESH = pl.DeviceIdType.MESH
NG = 72
PLANES = 9
PEERS = 8
FIELDS = 4
ROWS = 40
BLOCK = 184
LAST = 160
MERGED = NG * NG
WIDTH = 5248
OWN = 640
TAIL = PEERS * OWN
TAIL_OWNER = (0, 6)
FOLD = 11
MASKS = FOLD
QUARTERS = [(q * FOLD, min((q + 1) * FOLD, 41)) for q in range(4)]
TILES = WIDTH // 128
OWN_TILES = OWN // 128
TAIL_TILE = TILES - 1
coulomb_scale = 20.0
screening = 0.25
HALF = math.sqrt(0.5)


def dft8(x):
    a = [x[j] + x[j + 4] for j in range(4)]
    b = [x[j] - x[j + 4] for j in range(4)]
    e, o = a[0] + a[2], a[1] + a[3]
    u, v = HALF * (b[1] - b[3]), HALF * (b[1] + b[3])
    return [e + o, e - o, b[0] + u, v + b[2], a[0] - a[2], a[1] - a[3], b[0] - u, v - b[2]]


def dft8_adjoint(c):
    p, q = c[0] + c[1], c[0] - c[1]
    a = [p + c[4], q + c[5], p - c[4], q - c[5]]
    d, s = HALF * (c[2] - c[6]), HALF * (c[3] + c[7])
    b = [c[2] + c[6], d + s, c[3] - c[7], s - d]
    return [a[j] + b[j] for j in range(4)] + [a[j] - b[j] for j in range(4)]


def cos9(n):
    return math.cos(2.0 * math.pi * (n % 9) / 9)


def sin9(n):
    return math.sin(2.0 * math.pi * (n % 9) / 9)


def weighted(values, factors):
    total = values[0] * factors[0]
    for value, factor in zip(values[1:], factors[1:]):
        total = total + value * factor
    return total


def dft9(x):
    e = [x[n] + x[9 - n] for n in range(1, 5)]
    o = [x[n] - x[9 - n] for n in range(1, 5)]
    third = e[0] + e[1] + e[3]
    cosines = [x[0] + third + e[2]]
    sines = [None]
    for k in range(1, 5):
        if k == 3:
            cosines.append(x[0] + e[2] - 0.5 * third)
            sines.append(sin9(3) * (o[0] - o[1] + o[3]))
        else:
            cosines.append(x[0] + weighted(e, [cos9(k * n) for n in range(1, 5)]))
            sines.append(weighted(o, [sin9(k * n) for n in range(1, 5)]))
    return cosines, sines


def dft9_adjoint(cosines, sines):
    c, s = cosines, sines
    out = [None] * 9
    out[0] = c[0] + ((c[1] + c[2]) + (c[3] + c[4]))
    for n in range(1, 5):
        if n == 3:
            even = c[0] + c[3] - 0.5 * (c[1] + c[2] + c[4])
            odd = sin9(3) * (s[1] - s[2] + s[4])
        else:
            even = c[0] + weighted(c[1:], [cos9(k * n) for k in range(1, 5)])
            odd = weighted(s[1:], [sin9(k * n) for k in range(1, 5)])
        out[n] = even + odd
        out[9 - n] = even - odd
    return out


def finish72(load, save):
    for part in (0, 1):
        cosines, sines = dft9([load(part, b) for b in range(9)])
        base = part * 9
        save(base, cosines[0])
        for k in range(1, 5):
            save(base + 2 * k - 1, cosines[k])
            save(base + 2 * k, sines[k])
    for k8 in range(3):
        base = 18 + 18 * k8
        cc, cs = dft9([load(2 + 2 * k8, b) for b in range(9)])
        sc, ss = dft9([load(3 + 2 * k8, b) for b in range(9)])
        save(base, cc[0])
        save(base + 1, sc[0])
        for k in range(1, 5):
            at = base + 4 * k - 2
            save(at, cc[k] - ss[k])
            save(at + 1, cc[k] + ss[k])
            save(at + 2, sc[k] + cs[k])
            save(at + 3, sc[k] - cs[k])


def finish72_adjoint(load, save):
    for part in (0, 1):
        base = part * 9
        cosines = [load(base)] + [load(base + 2 * k - 1) for k in range(1, 5)]
        sines = [None] + [load(base + 2 * k) for k in range(1, 5)]
        for b, value in enumerate(dft9_adjoint(cosines, sines)):
            save(part, b, value)
    for k8 in range(3):
        base = 18 + 18 * k8
        cc, sc, cs, ss = [load(base)], [load(base + 1)], [None], [None]
        for k in range(1, 5):
            at = base + 4 * k - 2
            plus, minus, sine_plus, sine_minus = [load(at + i) for i in range(4)]
            cc.append(plus + minus)
            ss.append(minus - plus)
            sc.append(sine_plus + sine_minus)
            cs.append(sine_plus - sine_minus)
        for b, value in enumerate(dft9_adjoint(cc, cs)):
            save(2 + 2 * k8, b, value)
        for b, value in enumerate(dft9_adjoint(sc, ss)):
            save(3 + 2 * k8, b, value)


def point72(a, b):
    return (9 * a + 8 * b) % NG


def split(table):
    high = table.astype(ml_dtypes.bfloat16).astype(np.float64)
    return high, (table - high).astype(ml_dtypes.bfloat16).astype(np.float64)


def from_left(table):
    high, low = split(table)
    wide = np.zeros((80, 256))
    wide[:NG, : 3 * NG] = np.concatenate([high, high, low], axis=1)
    return wide


def from_right(table):
    high, low = split(table)
    return np.block([[high, low], [high, np.zeros_like(low)]])


@functools.cache
def tables():
    at = np.arange(NG)
    basis, freq = [np.full(NG, 1.0)], [0]
    for k in range(1, NG // 2):
        basis += [np.cos(2 * np.pi * k * at / NG), np.sin(2 * np.pi * k * at / NG)]
        freq += [k, k]
    basis.append(np.cos(np.pi * at))
    freq.append(NG // 2)
    basis = np.array(basis)
    basis /= np.sqrt((basis * basis).sum(1, keepdims=True))
    freq = np.array(freq, np.float64)
    eye = np.eye(NG)
    parts = [dft8([eye[point72(a, b)] for a in range(8)]) for b in range(9)]
    slots = [None] * NG
    finish72(lambda part, b: parts[b][part], slots.__setitem__)
    slots = np.array(slots)
    norm = (slots * slots).sum(1)
    spectrum = np.abs(np.fft.fft(slots, axis=1))[:, : NG // 2 + 1]
    freq_y = spectrum.argmax(1).astype(np.float64)
    along_z = np.zeros((128, 128))
    along_z[:NG, :NG] = basis.T
    along_x = basis.reshape(NG, PEERS, PLANES)
    along_x = np.concatenate([along_x[:, :, :8].reshape(NG, -1), along_x[:, :, 8]], axis=1)
    column = np.zeros((8, WIDTH), np.float32)
    column[0, :MERGED] = (freq_y[:, None] ** 2 + freq[None, :] ** 2).reshape(-1)
    column[1, :MERGED] = np.repeat(1.0 / norm, NG)
    freq_x = np.broadcast_to((freq**2)[:, None], (NG, 128)).astype(np.float32)
    wide = np.concatenate(
        [from_right(along_z), from_right(along_z.T), from_left(along_x), from_left(along_x.T)]
    )
    return wide.astype(ml_dtypes.bfloat16), column, freq_x


def take(load, start):
    tile, lane = divmod(start, 128)
    value = load(tile)
    if lane == 0:
        return value
    if lane + NG > 128:
        at = lax.broadcasted_iota(jnp.int32, value.shape, 1)
        value = jnp.where(at >= lane, value, load(tile + 1))
    return pltpu.roll(value, 128 - lane, 1)


def put(store, start, value):
    tile, lane = divmod(start, 128)
    if lane:
        value = pltpu.roll(value, lane, 1)
    end = min(lane + NG, 128)
    store(tile, slice(lane, end), value[:, lane:end])
    if lane + NG > 128:
        store(tile + 1, slice(0, lane + NG - 128), value[:, : lane + NG - 128])


def matmul(a, b):
    return jnp.dot(a, b, preferred_element_type=jnp.float32)


def halves(x):
    high = x.astype(jnp.bfloat16)
    return high, (x - high.astype(jnp.float32)).astype(jnp.bfloat16)


def left(table, x):
    high, low = [part.astype(jnp.float32) for part in halves(x)]
    zeros = jnp.zeros((8, x.shape[1]), jnp.float32)
    operand = jnp.concatenate([high, low, high, zeros], axis=0).astype(jnp.bfloat16)
    return matmul(table[:, 0 : operand.shape[0]], operand)[0:NG]


def kernel(
    bands,
    mask_ref,
    bands_hbm,
    wide_hbm,
    column_hbm,
    freq_hbm,
    out_ref,
    bands_ref,
    wide,
    column_ref,
    freq_ref,
    own,
    own_fold,
    visit,
    visit_fold,
    rho,
    work,
    work2,
    wave,
    wave_last,
    wave_tail,
    recv,
    recv_tail,
    back,
    back_tail,
    field,
    field_tail,
    relay,
    kernel_table,
    kernel_tail,
    total,
    total_fold,
    give,
    give_fold,
    given,
    given_fold,
    visit_send,
    visit_recv,
    give_send,
    give_recv,
    wave_send,
    wave_recv,
    tail_send,
    tail_recv,
    back_send,
    back_recv,
    back_tail_send,
    back_tail_recv,
    copy_sem,
    hop_send,
    hop_recv,
    forward_send,
    load_sem,
):
    me = lax.axis_index("pencil")
    group = lax.axis_index("band")
    me_x, me_y = lax.div(me, 4), lax.rem(me, 4)

    loads = [
        pltpu.make_async_copy(src, dst, load_sem.at[i])
        for i, (src, dst) in enumerate(
            [
                (bands_hbm, bands_ref),
                (wide_hbm, wide),
                (column_hbm, column_ref),
                (freq_hbm, freq_ref),
            ]
        )
    ]
    for load in loads:
        load.start()

    def peer(j):
        return lax.rem(me + j, PEERS)

    def at(dx, dy):
        return lax.rem(me_x + dx, 2) * 4 + lax.rem(me_y + dy + 4, 4)

    def group_at(j):
        return lax.rem(group + j + bands, bands)

    barrier = pltpu.get_barrier_semaphore()
    for j in range(1, PEERS):
        pl.semaphore_signal(barrier, inc=1, device_id={"pencil": peer(j)}, device_id_type=MESH)
    for j in (-2, -1, 1, 2):
        pl.semaphore_signal(barrier, inc=1, device_id={"band": group_at(j)}, device_id_type=MESH)
    loads[0].wait()
    for tile in range(TILES):
        lanes = slice(tile * 128, min(tile * 128 + 128, MERGED))
        live = slice(0, lanes.stop - lanes.start)
        if tile == TAIL_TILE:
            own[tile] = jnp.zeros((16, 128), jnp.float32)
            own_fold[tile % FOLD, 6:8, :] = jnp.zeros((2, 128), jnp.float32)
        for plane in range(PLANES - 1):
            own[tile, 2 * plane : 2 * plane + 2, live] = bands_ref[plane, :, lanes]
        row = tile // FOLD * 2
        own_fold[tile % FOLD, row : row + 2, live] = bands_ref[PLANES - 1, :, lanes]

    def own_mask(s, f):
        return mask_ref[0, s, f // 2, f % 2].astype(jnp.float32)

    for m in range(2 * FIELDS):
        value = own_mask(m // FIELDS, m % FIELDS)
        own_fold[MASKS, m : m + 1, :] = jnp.zeros((1, 128), jnp.float32) + value
    pl.semaphore_wait(barrier, PEERS - 1 + 4)

    def remote(src, dst, send, recv, **device):
        return pltpu.make_async_remote_copy(
            src_ref=src,
            dst_ref=dst,
            send_sem=send,
            recv_sem=recv,
            device_id=device,
            device_id_type=MESH,
        )

    odd = lax.rem(group, 2)
    even = odd == 0
    visitor_group = (
        jnp.where(even, group_at(2), group_at(1)),
        jnp.where(even, group_at(1), group_at(-2)),
    )

    def parts(main, fold):
        return [
            *(main.at[pl.ds(begin, end - begin)] for begin, end in QUARTERS),
            fold,
        ]

    def block_copies(src, dst, send, recv, to):
        return [
            remote(one, two, send.at[q], recv.at[q], band=to)
            for q, (one, two) in enumerate(zip(parts(*src), parts(*dst)))
        ]

    def visit_at(s):
        return visit.at[s], visit_fold.at[s]

    def visit_copies(s, src, send, to):
        return block_copies(src, visit_at(s), send, visit_recv.at[s], to)

    def lower_sends():
        return visit_copies(0, (own, own_fold), visit_send.at[0], group_at(-2))

    def lower_relays():
        return visit_copies(0, visit_at(0), visit_send.at[1], group_at(1))

    def upper_sends():
        return visit_copies(1, (own, own_fold), visit_send.at[0], group_at(2)) + visit_copies(
            1, (own, own_fold), visit_send.at[1], group_at(-1)
        )

    @pl.when(even)
    def _():
        for copy in lower_sends():
            copy.start()

    @pl.when(jnp.logical_not(even))
    def _():
        for copy in upper_sends():
            copy.start()

    def kernel_columns(start, width):
        squared = column_ref[0:1, pl.ds(start, width)]
        scale = column_ref[1:2, pl.ds(start, width)]
        return coulomb_scale / (freq_ref[:, 0:1] + squared + screening) * scale

    for load in loads[1:]:
        load.wait()
    kernel_table[...] = kernel_columns(pl.multiple_of(me * OWN, 128), OWN)
    kernel_tail[...] = kernel_columns(TAIL, 128)
    wave_tail[...] = jnp.zeros((2, ROWS, 128), jnp.float32)
    for s in range(2):
        for p in range(PEERS):
            back[s, (p + 1) * BLOCK - 8 : (p + 1) * BLOCK, :] = jnp.zeros((8, 128), jnp.float32)
            back_tail[s, (p + 1) * ROWS - 8 : (p + 1) * ROWS, :] = jnp.zeros((8, 128), jnp.float32)

    first_band = [pl.ds(band, 8, stride=2) for band in range(2)]
    field_rows = [pl.ds(f, 8, stride=FIELDS) for f in range(FIELDS)]
    row_at = lax.broadcasted_iota(jnp.int32, (8, 128), 0)
    resident_one = lax.rem(lax.div(row_at, 2), 2) == 1
    visitor_one = lax.rem(row_at, 2) == 1

    def last_planes(s, j, q):
        a = [own_fold[j, 2 * q + band : 2 * q + band + 1, :] for band in range(2)]
        c = [visit_fold[s, j, 2 * q + band : 2 * q + band + 1, :] for band in range(2)]
        wide_a = [jnp.broadcast_to(row, (8, 128)) for row in a]
        wide_c = [jnp.broadcast_to(row, (8, 128)) for row in c]
        return (
            jnp.where(resident_one, wide_a[1], wide_a[0]),
            jnp.where(visitor_one, wide_c[1], wide_c[0]),
        )

    def along_z(start):
        table = wide[start : start + 256, :]

        def step(i, carry):
            rows = pl.ds(pl.multiple_of(i * 720, 720), 720)
            both = matmul(jnp.concatenate(halves(work[rows, :]), axis=1), table)
            work2[rows, :] = both[:, :128] + both[:, 128:]
            return carry

        lax.fori_loop(0, NG * ROWS // 720, step, 0)

    def place(part, b, t):
        return pl.ds(pl.multiple_of((part * 9 + b) * ROWS + t * 8, 8), 8)

    def first(s):
        arriving = visit_copies(s, (own, own_fold), visit_send.at[0], group_at(1))
        arriving[4].wait_recv()
        relays = lower_relays()
        if s == 0:

            @pl.when(even)
            def _():
                relays[4].start()

        for q, (begin, end) in enumerate(QUARTERS):
            arriving[q].wait_recv()
            if s == 0:

                @pl.when(even)
                def _(q=q):
                    relays[q].start()

            def products(j, carry, q=q, begin=begin):
                tile = begin + j
                phi = [own[tile, rows, :] for rows in first_band]
                chi = [visit[s, tile, rows, :] for rows in first_band]
                for f in range(FIELDS):
                    rho[tile, field_rows[f], :] = phi[f // 2] * chi[f % 2]
                phi, chi = last_planes(s, j, q)
                rho[tile, 32:40, :] = phi * chi
                return carry

            lax.fori_loop(0, end - begin, products, 0, unroll=True)
        for b in range(9):
            starts = [point72(a, b) * NG for a in range(8)]
            parts = dft8([take(lambda i: rho[i], at) for at in starts])
            for part in range(8):
                base = (part * 9 + b) * ROWS
                work[base : base + ROWS, :] = parts[part]
        along_z(0)

        def finish(t, target):
            def load(part, b):
                return work2[place(part, b, t), :]

            def save(slot, value):
                put(target, slot * NG, value)

            finish72(load, save)

        def planes(t, carry):
            def target(tile, lanes, piece):
                if tile == TAIL_TILE:
                    wave_tail[s, pl.ds(pl.multiple_of(t * 8, 8), 8), lanes] = piece
                else:
                    start = tile // OWN_TILES * BLOCK + tile % OWN_TILES * 32
                    wave[s, pl.ds(pl.multiple_of(start + t * 8, 8), 8), lanes] = piece

            finish(t, target)
            return carry

        lax.fori_loop(0, 4, planes, 0)

        def last(tile, lanes, piece):
            if tile == TAIL_TILE:
                wave_tail[s, 32:40, lanes] = piece
            else:
                wave_last[tile * 8 : tile * 8 + 8, lanes] = piece

        finish(4, last)
        upper = lax.broadcasted_iota(jnp.int32, (8, 128), 0) < FIELDS
        for q in range(PEERS):
            for i in range(3):
                tile = (q * OWN_TILES + i) * 8
                piece = wave_last[tile : tile + 8, :]
                if i < 2:
                    piece = jnp.where(upper, piece, wave_last[tile + 24 : tile + 32, :])
                start = q * BLOCK + LAST + i * 8
                wave[s, start : start + 8, :] = piece

    def block_of(ref, s, index):
        return ref.at[s, pl.ds(pl.multiple_of(index * BLOCK, 8), BLOCK), :]

    def tail_of(ref, s, index):
        return ref.at[s, pl.ds(pl.multiple_of(index * ROWS, 8), ROWS), :]

    way = jnp.where(even, 1, -1)
    exchange_refs = ((wave, recv, wave_send, wave_recv), (back, field, back_send, back_recv))

    def hop(phase, s, dx):
        return remote(
            block_of(exchange_refs[phase][0], s, at(dx, 2)),
            relay.at[phase, s, dx],
            hop_send.at[phase, s, dx],
            hop_recv.at[phase, s, dx],
            pencil=at(dx, way),
        )

    def forward(phase, s, dx):
        return remote(
            relay.at[phase, s, dx],
            block_of(exchange_refs[phase][1], s, at(dx, -way)),
            forward_send.at[phase, s, dx],
            exchange_refs[phase][3].at[s, dx * 4 + 2],
            pencil=at(0, way),
        )

    def direct(phase, s, dx, dy):
        src, dst, send, recv_sem = exchange_refs[phase]
        return remote(
            block_of(src, s, at(dx, dy)),
            block_of(dst, s, me),
            send.at[s, dx * 4 + dy],
            recv_sem.at[s, dx * 4 + dy],
            pencil=at(dx, dy),
        )

    straight = [(1, 1), (1, 3), (0, 1), (0, 3), (1, 0)]

    def keep(phase, s):
        src, dst = exchange_refs[phase][:2]
        return pltpu.make_async_copy(
            block_of(src, s, me), block_of(dst, s, me), copy_sem.at[phase, s]
        )

    def send_blocks(phase, s):
        for dx in range(2):
            hop(phase, s, dx).start()
        for dx, dy in straight:
            direct(phase, s, dx, dy).start()
        keep(phase, s).start()

    def forward_blocks(phase, s):
        for dx in range(2):
            hop(phase, s, dx).wait_recv()
            forward(phase, s, dx).start()

    def wait_blocks(phase, s):
        keep(phase, s).wait()
        for dx, dy in straight:
            direct(phase, s, dx, dy).wait_recv()
        for dx in range(2):
            forward(phase, s, dx).wait_recv()

    def end_blocks(phase, s):
        for dx, dy in straight:
            direct(phase, s, dx, dy).wait_send()
        for dx in range(2):
            hop(phase, s, dx).wait_send()
            forward(phase, s, dx).wait_send()

    def tail_copy(s):
        owner = TAIL_OWNER[s]
        distance = lax.rem(owner - me + PEERS, PEERS)
        return remote(
            wave_tail.at[s],
            tail_of(recv_tail, s, me),
            tail_send.at[s],
            tail_recv.at[s, distance],
            pencil=jnp.int32(owner),
        )

    def lines(f, tile, block, last):
        first_rows = [
            pl.ds(p * block + tile * 32 + f, 8, stride=FIELDS) for p in range(PEERS)
        ]
        below = FIELDS * (tile // 3)
        return first_rows + [pl.ds(last + tile % 3 * 8 + below + f, PEERS, stride=block)]

    def spectrum_step(source, target, s, tiles, table, block, last):
        columns = slice(tiles[0] * 128, (tiles[-1] + 1) * 128)
        for f in range(FIELDS):
            rows = [lines(f, tile, block, last) for tile in tiles]
            loaded = [
                jnp.concatenate([source[s, part, :] for part in parts], axis=0) for parts in rows
            ]
            spectrum = left(wide[512:592, :], jnp.concatenate(loaded, axis=1))
            result = left(wide[592:672, :], spectrum * table[:, columns])
            for i, parts in enumerate(rows):
                for j, part in enumerate(parts):
                    target[s, part, :] = result[j * 8 : j * 8 + 8, i * 128 : (i + 1) * 128]

    def second(s):
        spectrum_step(recv, back, s, range(OWN_TILES), kernel_table, BLOCK, LAST)

    def give_copies(s):
        return block_copies(
            (give.at[s], give_fold.at[s]),
            (given.at[odd], given_fold.at[odd]),
            give_send.at[s],
            give_recv.at[odd],
            visitor_group[s],
        )

    def given_copies(source):
        return block_copies(
            (give.at[0], give_fold.at[0]),
            (given.at[source], given_fold.at[source]),
            give_send.at[0],
            give_recv.at[source],
            visitor_group[0],
        )

    def third(s):
        def start(t, source):
            def load(slot):
                return take(source, slot * NG)

            def save(part, b, value):
                work[place(part, b, t), :] = value

            finish72_adjoint(load, save)

        def planes(t, carry):
            def source(tile):
                if tile == TAIL_TILE:
                    return field_tail[s, pl.ds(pl.multiple_of(t * 8, 8), 8), :]
                first_row = tile // OWN_TILES * BLOCK + tile % OWN_TILES * 32
                return field[s, pl.ds(pl.multiple_of(first_row + t * 8, 8), 8), :]

            start(t, source)
            return carry

        lax.fori_loop(0, 4, planes, 0)

        def last(tile):
            if tile == TAIL_TILE:
                return field_tail[s, 32:40, :]
            which = tile % OWN_TILES
            first_row = tile // OWN_TILES * BLOCK + LAST + which % 3 * 8
            value = field[s, first_row : first_row + 8, :]
            return pltpu.roll(value, FIELDS, 0) if which > 2 else value

        start(4, last)
        along_z(256)
        for b in range(9):
            parts = []
            for part in range(8):
                base = (part * 9 + b) * ROWS
                parts.append(work2[base : base + ROWS, :])
            for a, value in enumerate(dft8_adjoint(parts)):


                def store(tile, lanes, piece):
                    rho[tile, :, lanes] = piece

                put(store, point72(a, b) * NG, value)
        weights = []
        for f in range(FIELDS):
            g = 2 * (f % 2) + f // 2
            if s == 0:
                row = jnp.where(
                    even,
                    visit_fold[s, MASKS, FIELDS + g : FIELDS + g + 1, :],
                    visit_fold[s, MASKS, g : g + 1, :],
                )
            else:
                row = jnp.where(
                    even,
                    visit_fold[s, MASKS, g : g + 1, :],
                    own_fold[MASKS, FIELDS + f : FIELDS + f + 1, :],
                )
            weights.append(jnp.broadcast_to(row, (8, 128)))
        last_weight = weights[3]
        for f in range(3):
            last_weight = jnp.where(row_at == f, weights[f], last_weight)

        leaving = give_copies(s)
        for q, (begin, end) in enumerate(QUARTERS):

            def gather(j, carry, q=q, begin=begin):
                tile = begin + j
                phi = [own[tile, rows, :] for rows in first_band]
                chi = [visit[s, tile, rows, :] for rows in first_band]
                value = [rho[tile, field_rows[f], :] * weights[f] for f in range(FIELDS)]
                for a in range(2):
                    stay = value[2 * a] * chi[0] + value[2 * a + 1] * chi[1]
                    if s > 0:
                        stay = stay + total[tile, first_band[a], :]
                    total[tile, first_band[a], :] = stay
                for c in range(2):
                    give[s, tile, first_band[c], :] = value[c] * phi[0] + value[2 + c] * phi[1]
                phi, chi = last_planes(s, j, q)
                value = rho[tile, 32:40, :] * last_weight
                stay, leave = value * chi, value * phi
                stay = stay + pltpu.roll(stay, 7, 0)
                leave = leave + pltpu.roll(leave, 6, 0)
                for band in range(2):
                    row = slice(2 * q + band, 2 * q + band + 1)
                    kept = stay[2 * band : 2 * band + 1]
                    if s > 0:
                        kept = kept + total_fold[j, row, :]
                    total_fold[j, row, :] = kept
                    give_fold[s, j, row, :] = leave[band : band + 1]
                return carry

            lax.fori_loop(0, end - begin, gather, 0, unroll=True)
            leaving[q].start()
        leaving[4].start()

    def tail_back(s, j):
        return remote(
            tail_of(back_tail, s, peer(j)),
            field_tail.at[s],
            back_tail_send.at[s, j],
            back_tail_recv.at[s],
            pencil=peer(j),
        )

    def send_tail(s):
        owner = TAIL_OWNER[s]

        @pl.when(me == owner)
        def _():
            recv_tail[s, owner * ROWS : (owner + 1) * ROWS, :] = wave_tail[s]

        @pl.when(me != owner)
        def _():
            tail_copy(s).start()

    def turn_tail(s):
        owner = TAIL_OWNER[s]

        @pl.when(me == owner)
        def _():
            for j in range(1, PEERS):
                remote(
                    wave_tail.at[s],
                    tail_of(recv_tail, s, me),
                    tail_send.at[s],
                    tail_recv.at[s, j],
                    pencil=peer(j),
                ).wait_recv()
            spectrum_step(recv_tail, back_tail, s, (0,), kernel_tail, ROWS, 32)
            for j in range(1, PEERS):
                tail_back(s, j).start()
            field_tail[s] = back_tail[s, owner * ROWS : (owner + 1) * ROWS, :]

    def end_tail(s):
        owner = TAIL_OWNER[s]

        @pl.when(me == owner)
        def _():
            for j in range(1, PEERS):
                tail_back(s, j).wait_send()

        @pl.when(me != owner)
        def _():
            tail_copy(s).wait_send()
            tail_back(s, 1).wait_recv()

    for s in range(2):
        first(s)
        if s == 1:
            forward_blocks(0, 0)
        send_blocks(0, s)
        send_tail(s)
    for s in range(2):
        wait_blocks(0, s)
        second(s)
        send_blocks(1, s)
        turn_tail(s)
        if s == 0:
            forward_blocks(0, 1)
            forward_blocks(1, 0)
    for s in range(2):
        wait_blocks(1, s)
        end_tail(s)
        third(s)
        if s == 0:
            forward_blocks(1, 1)
    for q, (begin, end) in enumerate(QUARTERS):
        for source in range(2):
            given_copies(source)[q].wait_recv()
        for tile in range(begin, end):
            lanes = slice(tile * 128, min(tile * 128 + 128, MERGED))
            term = -(total[tile] + given[0, tile] + given[1, tile])
            for plane in range(PLANES - 1):
                piece = term[2 * plane : 2 * plane + 2, 0 : lanes.stop - lanes.start]
                out_ref[plane, :, lanes] = piece
    for source in range(2):
        given_copies(source)[4].wait_recv()
    for q, (begin, end) in enumerate(QUARTERS):
        for tile in range(begin, end):
            lanes = slice(tile * 128, min(tile * 128 + 128, MERGED))
            j, rows = tile - begin, slice(2 * q, 2 * q + 2)
            term = total_fold[j, rows, :] + given_fold[0, j, rows, :] + given_fold[1, j, rows, :]
            out_ref[PLANES - 1, :, lanes] = -term[:, 0 : lanes.stop - lanes.start]

    @pl.when(even)
    def _():
        for copy in lower_sends() + lower_relays():
            copy.wait_send()

    @pl.when(jnp.logical_not(even))
    def _():
        for copy in upper_sends():
            copy.wait_send()

    for s in range(2):
        for copy in give_copies(s):
            copy.wait_send()
    for phase in range(2):
        for s in range(2):
            end_blocks(phase, s)


def body(bands, orbitals, pair_mask):
    hbm = pl.BlockSpec(memory_space=pltpu.HBM)
    smem = pl.BlockSpec(memory_space=pltpu.SMEM)
    consts = [jnp.asarray(table) for table in tables()]
    dma = pltpu.SemaphoreType.DMA

    def buffer(*shape):
        return pltpu.VMEM(shape, jnp.float32)

    out = pl.pallas_call(
        functools.partial(kernel, bands),
        out_shape=jax.ShapeDtypeStruct((PLANES, 2, MERGED), jnp.float32),
        in_specs=[smem] + [hbm] * (1 + len(consts)),
        out_specs=pl.BlockSpec(memory_space=pltpu.VMEM),
        scratch_shapes=[
            buffer(PLANES, 2, MERGED),
            pltpu.VMEM(consts[0].shape, jnp.bfloat16),
            buffer(*consts[1].shape),
            buffer(*consts[2].shape),
            buffer(TILES, 16, 128),
            buffer(FOLD + 1, 8, 128),
            buffer(2, TILES, 16, 128),
            buffer(2, FOLD + 1, 8, 128),
            buffer(TILES, ROWS, 128),
            buffer(NG * ROWS, 128),
            buffer(NG * ROWS, 128),
            buffer(2, PEERS * BLOCK, 128),
            buffer(TAIL_TILE * 8, 128),
            buffer(2, ROWS, 128),
            buffer(2, PEERS * BLOCK, 128),
            buffer(2, PEERS * ROWS, 128),
            buffer(2, PEERS * BLOCK, 128),
            buffer(2, PEERS * ROWS, 128),
            buffer(2, PEERS * BLOCK, 128),
            buffer(2, ROWS, 128),
            buffer(2, 2, 2, BLOCK, 128),
            buffer(NG, OWN),
            buffer(NG, 128),
            buffer(TILES, 16, 128),
            buffer(FOLD + 1, 8, 128),
            buffer(2, TILES, 16, 128),
            buffer(2, FOLD + 1, 8, 128),
            buffer(2, TILES, 16, 128),
            buffer(2, FOLD + 1, 8, 128),
            dma((2, 5)),
            dma((2, 5)),
            dma((2, 5)),
            dma((2, 5)),
            dma((2, PEERS)),
            dma((2, PEERS)),
            dma((2,)),
            dma((2, PEERS)),
            dma((2, PEERS)),
            dma((2, PEERS)),
            dma((2, PEERS)),
            dma((2,)),
            dma((2, 2)),
            dma((2, 2, 2)),
            dma((2, 2, 2)),
            dma((2, 2, 2)),
            dma((4,)),
        ],
        compiler_params=pltpu.CompilerParams(
            collective_id=0, has_side_effects=True, vmem_limit_bytes=64 * 1024 * 1024 - 65536
        ),
    )(pair_mask, orbitals.transpose(1, 0, 2), *consts)
    return out.transpose(1, 0, 2)


def solution(mesh):
    return jax.shard_map(
        functools.partial(body, mesh.shape["band"]),
        mesh=mesh,
        in_specs=(P("band", "pencil", None), P("band", None, None, None)),
        out_specs=P("band", "pencil", None),
        check_vma=False,
    )
```

profile of v0, /device:TPU:217, one launch (start us, length us, event | category | flops | bytes accessed | tf_op | source)
XLA Modules:
  0.0 68.9 jit_solution(17816617807848454262)
XLA Ops:
  0.0 67.1 %shard_map.55 = f32[9,2,5184]{2,1,0:T(2,128)} custom-call(s32[1,2,2,2]{3,2,1,0:T(2,128)} %mask_ref.1, f32[9,2,5184]{2,1,0:T(2,128)} %bitcast.3, bf16[672,256]{1,0:T(8,128)(2,1)} %constant.6.clone.wide_hbm, f32[8,5248]{1,0:T(8,128)} %constant.7.clone.column_hbm, f32[72,128]{1,0:T(8,128)} %constant.8.clone.freq_hbm), custom_call_target="tpu_custom_call" | custom-call | tf_op jit(solution)/shard_map/pallas_call | solution.py:857
  67.1 1.8 %copy.7 = f32[2,9,5184]{2,0,1:T(2,128)} copy(f32[2,9,5184]{2,0,1:T(2,128)} %bitcast.2) | data formatting | bytes 746496
where the time goes:
time: 69 us; the launch traced here: 68.9 us
  Pallas kernels  67.1 us (97%)
  local copies, waits for them, and re-layouts  1.76 us (3%)
    pallas_call x1, Pallas kernels, body(): pl.pallas_call(functools.partial(kernel, bands), out_shape=jax.ShapeDtype...  67.1 us
    unnamed x1, local copies, waits for them, and re-layouts  1.76 us

commit v1 on v0

--- a/solution.py
+++ b/solution.py
@@ -22,7 +22,7 @@
 WIDTH = 5248
 OWN = 640
 TAIL = PEERS * OWN
-TAIL_OWNER = (0, 6)
+PIECE = 16
 FOLD = 11
 MASKS = FOLD
 QUARTERS = [(q * FOLD, min((q + 1) * FOLD, 41)) for q in range(4)]
@@ -246,6 +246,7 @@
     wide,
     column_ref,
     freq_ref,
+    mixed,
     own,
     own_fold,
     visit,
@@ -256,12 +257,14 @@
     wave,
     wave_last,
     wave_tail,
+    wave_piece,
     recv,
     recv_tail,
     back,
     back_tail,
     field,
     field_tail,
+    field_piece,
     relay,
     kernel_table,
     kernel_tail,
@@ -326,10 +329,12 @@
         lanes = slice(tile * 128, min(tile * 128 + 128, MERGED))
         live = slice(0, lanes.stop - lanes.start)
         if tile == TAIL_TILE:
-            own[tile] = jnp.zeros((16, 128), jnp.float32)
+            mixed[tile] = jnp.zeros((16, 128), jnp.float32)
             own_fold[tile % FOLD, 6:8, :] = jnp.zeros((2, 128), jnp.float32)
         for plane in range(PLANES - 1):
-            own[tile, 2 * plane : 2 * plane + 2, live] = bands_ref[plane, :, lanes]
+            mixed[tile, 2 * plane : 2 * plane + 2, live] = bands_ref[plane, :, lanes]
+        for band in range(2):
+            own[tile, band * 8 : band * 8 + 8, :] = mixed[tile, pl.ds(band, 8, stride=2), :]
         row = tile // FOLD * 2
         own_fold[tile % FOLD, row : row + 2, live] = bands_ref[PLANES - 1, :, lanes]
 
@@ -410,10 +415,13 @@
     for s in range(2):
         for p in range(PEERS):
             back[s, (p + 1) * BLOCK - 8 : (p + 1) * BLOCK, :] = jnp.zeros((8, 128), jnp.float32)
-            back_tail[s, (p + 1) * ROWS - 8 : (p + 1) * ROWS, :] = jnp.zeros((8, 128), jnp.float32)
-
-    first_band = [pl.ds(band, 8, stride=2) for band in range(2)]
-    field_rows = [pl.ds(f, 8, stride=FIELDS) for f in range(FIELDS)]
+            back_tail[s, (p + 1) * PIECE - 8 : (p + 1) * PIECE, :] = jnp.zeros((8, 128), jnp.float32)
+        field_tail[s, 32:40, :] = jnp.zeros((8, 128), jnp.float32)
+        for f in range(FIELDS):
+            wave_piece[s, f, 8:16, :] = jnp.zeros((8, 128), jnp.float32)
+
+    first_band = [slice(band * 8, band * 8 + 8) for band in range(2)]
+    field_rows = [slice(f * 8, f * 8 + 8) for f in range(FIELDS)]
     row_at = lax.broadcasted_iota(jnp.int32, (8, 128), 0)
     resident_one = lax.rem(lax.div(row_at, 2), 2) == 1
     visitor_one = lax.rem(row_at, 2) == 1
@@ -442,7 +450,7 @@
     def place(part, b, t):
         return pl.ds(pl.multiple_of((part * 9 + b) * ROWS + t * 8, 8), 8)
 
-    def first(s):
+    def first(s, between):
         arriving = visit_copies(s, (own, own_fold), visit_send.at[0], group_at(1))
         arriving[4].wait_recv()
         relays = lower_relays()
@@ -478,6 +486,7 @@
                 base = (part * 9 + b) * ROWS
                 work[base : base + ROWS, :] = parts[part]
         along_z(0)
+        between()
 
         def finish(t, target):
             def load(part, b):
@@ -508,6 +517,9 @@
                 wave_last[tile * 8 : tile * 8 + 8, lanes] = piece
 
         finish(4, last)
+        for f in range(FIELDS):
+            wave_piece[s, f, 0:8, :] = wave_tail[s, field_rows[f], :]
+            wave_piece[s, f, 8:9, :] = wave_tail[s, 32 + f : 33 + f, :]
         upper = lax.broadcasted_iota(jnp.int32, (8, 128), 0) < FIELDS
         for q in range(PEERS):
             for i in range(3):
@@ -589,27 +601,29 @@
             hop(phase, s, dx).wait_send()
             forward(phase, s, dx).wait_send()
 
-    def tail_copy(s):
-        owner = TAIL_OWNER[s]
-        distance = lax.rem(owner - me + PEERS, PEERS)
+    def piece_of(ref, s, index):
+        return ref.at[s, pl.ds(pl.multiple_of(index * PIECE, 8), PIECE), :]
+
+    def owner_of(s, f):
+        return FIELDS * s + f
+
+    def tail_copy(s, f, distance):
         return remote(
-            wave_tail.at[s],
-            tail_of(recv_tail, s, me),
-            tail_send.at[s],
+            wave_piece.at[s, f],
+            piece_of(recv_tail, s, me),
+            tail_send.at[s, f],
             tail_recv.at[s, distance],
-            pencil=jnp.int32(owner),
+            pencil=jnp.int32(owner_of(s, f)),
         )
 
     def lines(f, tile, block, last):
-        first_rows = [
-            pl.ds(p * block + tile * 32 + f, 8, stride=FIELDS) for p in range(PEERS)
-        ]
+        first_rows = [pl.ds(p * block + tile * 32 + f * 8, 8) for p in range(PEERS)]
         below = FIELDS * (tile // 3)
         return first_rows + [pl.ds(last + tile % 3 * 8 + below + f, PEERS, stride=block)]
 
-    def spectrum_step(source, target, s, tiles, table, block, last):
+    def spectrum_step(source, target, s, tiles, table, block, last, fields):
         columns = slice(tiles[0] * 128, (tiles[-1] + 1) * 128)
-        for f in range(FIELDS):
+        for f in fields:
             rows = [lines(f, tile, block, last) for tile in tiles]
             loaded = [
                 jnp.concatenate([source[s, part, :] for part in parts], axis=0) for parts in rows
@@ -620,8 +634,12 @@
                 for j, part in enumerate(parts):
                     target[s, part, :] = result[j * 8 : j * 8 + 8, i * 128 : (i + 1) * 128]
 
-    def second(s):
-        spectrum_step(recv, back, s, range(OWN_TILES), kernel_table, BLOCK, LAST)
+    def second(s, between):
+        for half in range(2):
+            fields = range(2 * half, 2 * half + 2)
+            spectrum_step(recv, back, s, range(OWN_TILES), kernel_table, BLOCK, LAST, fields)
+            if half == 0:
+                between()
 
     def give_copies(s):
         return block_copies(
@@ -641,7 +659,7 @@
             visitor_group[0],
         )
 
-    def third(s):
+    def third(s, between):
         def start(t, source):
             def load(slot):
                 return take(source, slot * NG)
@@ -673,6 +691,7 @@
 
         start(4, last)
         along_z(256)
+        between()
         for b in range(9):
             parts = []
             for part in range(8):
@@ -738,85 +757,102 @@
             leaving[q].start()
         leaving[4].start()
 
-    def tail_back(s, j):
+    def tail_back(s, f, j):
         return remote(
-            tail_of(back_tail, s, peer(j)),
-            field_tail.at[s],
+            piece_of(back_tail, s, peer(j)),
+            field_piece.at[s, f],
             back_tail_send.at[s, j],
-            back_tail_recv.at[s],
+            back_tail_recv.at[s, f],
             pencil=peer(j),
         )
 
     def send_tail(s):
-        owner = TAIL_OWNER[s]
-
-        @pl.when(me == owner)
-        def _():
-            recv_tail[s, owner * ROWS : (owner + 1) * ROWS, :] = wave_tail[s]
-
-        @pl.when(me != owner)
-        def _():
-            tail_copy(s).start()
+        for f in range(FIELDS):
+            owner = owner_of(s, f)
+
+            @pl.when(me == owner)
+            def _(f=f, owner=owner):
+                recv_tail[s, owner * PIECE : (owner + 1) * PIECE, :] = wave_piece[s, f]
+
+            @pl.when(me != owner)
+            def _(f=f, owner=owner):
+                tail_copy(s, f, lax.rem(owner - me + PEERS, PEERS)).start()
 
     def turn_tail(s):
-        owner = TAIL_OWNER[s]
-
-        @pl.when(me == owner)
+        owned = lax.div(me, FIELDS) == s
+
+        @pl.when(owned)
         def _():
             for j in range(1, PEERS):
-                remote(
-                    wave_tail.at[s],
-                    tail_of(recv_tail, s, me),
-                    tail_send.at[s],
-                    tail_recv.at[s, j],
-                    pencil=peer(j),
-                ).wait_recv()
-            spectrum_step(recv_tail, back_tail, s, (0,), kernel_tail, ROWS, 32)
+                tail_copy(s, 0, j).wait_recv()
+            parts = [pl.ds(p * PIECE, 8) for p in range(PEERS)] + [pl.ds(8, PEERS, stride=PIECE)]
+            block = jnp.concatenate([recv_tail[s, part, :] for part in parts], axis=0)
+            spectrum = left(wide[512:592, :], block) * kernel_tail[...]
+            result = left(wide[592:672, :], spectrum)
+            for i, part in enumerate(parts):
+                back_tail[s, part, :] = result[i * 8 : i * 8 + 8, :]
+            mine = lax.rem(me, FIELDS)
             for j in range(1, PEERS):
-                tail_back(s, j).start()
-            field_tail[s] = back_tail[s, owner * ROWS : (owner + 1) * ROWS, :]
+                tail_back(s, mine, j).start()
+            field_piece[s, mine] = back_tail[s, pl.ds(pl.multiple_of(me * PIECE, 8), PIECE), :]
 
     def end_tail(s):
-        owner = TAIL_OWNER[s]
-
-        @pl.when(me == owner)
+        for f in range(FIELDS):
+            owner = owner_of(s, f)
+
+            @pl.when(me != owner)
+            def _(f=f, owner=owner):
+                tail_copy(s, f, lax.rem(owner - me + PEERS, PEERS)).wait_send()
+                tail_back(s, f, 1).wait_recv()
+
+            field_tail[s, field_rows[f], :] = field_piece[s, f, 0:8, :]
+            field_tail[s, 32 + f : 33 + f, :] = field_piece[s, f, 8:9, :]
+
+        @pl.when(lax.div(me, FIELDS) == s)
         def _():
             for j in range(1, PEERS):
-                tail_back(s, j).wait_send()
-
-        @pl.when(me != owner)
-        def _():
-            tail_copy(s).wait_send()
-            tail_back(s, 1).wait_recv()
-
-    for s in range(2):
-        first(s)
-        if s == 1:
-            forward_blocks(0, 0)
-        send_blocks(0, s)
-        send_tail(s)
-    for s in range(2):
-        wait_blocks(0, s)
-        second(s)
-        send_blocks(1, s)
-        turn_tail(s)
-        if s == 0:
-            forward_blocks(0, 1)
-            forward_blocks(1, 0)
-    for s in range(2):
-        wait_blocks(1, s)
-        end_tail(s)
-        third(s)
-        if s == 0:
-            forward_blocks(1, 1)
+                tail_back(s, lax.rem(me, FIELDS), j).wait_send()
+
+    def nothing():
+        pass
+
+    def forwards(*which):
+        def run():
+            for phase, s in which:
+                forward_blocks(phase, s)
+
+        return run
+
+    first(0, nothing)
+    send_blocks(0, 0)
+    send_tail(0)
+    first(1, forwards((0, 0)))
+    send_blocks(0, 1)
+    send_tail(1)
+    wait_blocks(0, 0)
+    second(0, forwards((0, 1)))
+    send_blocks(1, 0)
+    turn_tail(0)
+    wait_blocks(0, 1)
+    second(1, forwards((1, 0)))
+    send_blocks(1, 1)
+    turn_tail(1)
+    wait_blocks(1, 0)
+    end_tail(0)
+    third(0, forwards((1, 1)))
+    wait_blocks(1, 1)
+    end_tail(1)
+    third(1, nothing)
     for q, (begin, end) in enumerate(QUARTERS):
         for source in range(2):
             given_copies(source)[q].wait_recv()
         for tile in range(begin, end):
             lanes = slice(tile * 128, min(tile * 128 + 128, MERGED))
-            term = -(total[tile] + given[0, tile] + given[1, tile])
+            for rows, band in zip(first_band, range(2)):
+                term = -(total[tile, rows, :] + given[0, tile, rows, :] + given[1, tile, rows, :])
+                mixed[tile, pl.ds(band, 8, stride=2), :] = term
             for plane in range(PLANES - 1):
-                piece = term[2 * plane : 2 * plane + 2, 0 : lanes.stop - lanes.start]
+                piece = mixed[tile, 2 * plane : 2 * plane + 2, 0 : lanes.stop - lanes.start]
                 out_ref[plane, :, lanes] = piece
     for source in range(2):
         given_copies(source)[4].wait_recv()
@@ -865,6 +901,7 @@
             buffer(*consts[1].shape),
             buffer(*consts[2].shape),
             buffer(TILES, 16, 128),
+            buffer(TILES, 16, 128),
             buffer(FOLD + 1, 8, 128),
             buffer(2, TILES, 16, 128),
             buffer(2, FOLD + 1, 8, 128),
@@ -874,12 +911,14 @@
             buffer(2, PEERS * BLOCK, 128),
             buffer(TAIL_TILE * 8, 128),
             buffer(2, ROWS, 128),
+            buffer(2, FIELDS, PIECE, 128),
             buffer(2, PEERS * BLOCK, 128),
-            buffer(2, PEERS * ROWS, 128),
+            buffer(2, PEERS * PIECE, 128),
             buffer(2, PEERS * BLOCK, 128),
-            buffer(2, PEERS * ROWS, 128),
+            buffer(2, PEERS * PIECE, 128),
             buffer(2, PEERS * BLOCK, 128),
             buffer(2, ROWS, 128),
+            buffer(2, FIELDS, PIECE, 128),
             buffer(2, 2, 2, BLOCK, 128),
             buffer(NG, OWN),
             buffer(NG, 128),
@@ -895,12 +934,12 @@
             dma((2, 5)),
             dma((2, PEERS)),
             dma((2, PEERS)),
-            dma((2,)),
+            dma((2, FIELDS)),
             dma((2, PEERS)),
             dma((2, PEERS)),
             dma((2, PEERS)),
             dma((2, PEERS)),
-            dma((2,)),
+            dma((2, FIELDS)),
             dma((2, 2)),
             dma((2, 2, 2)),
             dma((2, 2, 2)),

time: 69 us -> 68.8 us (level)
  the two profiles are of different devices: /device:TPU:217 before, /device:TPU:24 now
where the time goes in v1:
time: 68.8 us; the launch traced here: 68.7 us
  Pallas kernels  66.9 us (97%)
  local copies, waits for them, and re-layouts  1.76 us (3%)
    pallas_call x1, Pallas kernels, body(): pl.pallas_call(functools.partial(kernel, bands), out_shape=jax.ShapeDtype...  66.9 us
    unnamed x1, local copies, waits for them, and re-layouts  1.76 us

profile of v1, /device:TPU:24, one launch (start us, length us, event | category | flops | bytes accessed | tf_op | source)
XLA Modules:
  0.0 68.7 jit_solution(3096262040554551108)
XLA Ops:
  0.0 66.9 %shard_map.55 = f32[9,2,5184]{2,1,0:T(2,128)} custom-call(s32[1,2,2,2]{3,2,1,0:T(2,128)} %mask_ref.1, f32[9,2,5184]{2,1,0:T(2,128)} %bitcast.3, bf16[672,256]{1,0:T(8,128)(2,1)} %constant.6.clone.wide_hbm, f32[8,5248]{1,0:T(8,128)} %constant.7.clone.column_hbm, f32[72,128]{1,0:T(8,128)} %constant.8.clone.freq_hbm), custom_call_target="tpu_custom_call" | custom-call | tf_op jit(solution)/shard_map/pallas_call | solution.py:893
  66.9 1.8 %copy.7 = f32[2,9,5184]{2,0,1:T(2,128)} copy(f32[2,9,5184]{2,0,1:T(2,128)} %bitcast.2) | data formatting | bytes 746496

commit v2 on v1

--- a/solution.py
+++ b/solution.py
@@ -16,8 +16,8 @@
 PEERS = 8
 FIELDS = 4
 ROWS = 40
-BLOCK = 184
-LAST = 160
+PART = 40
+LAST = 24
 MERGED = NG * NG
 WIDTH = 5248
 OWN = 640
@@ -255,17 +255,20 @@
     work,
     work2,
     wave,
+    wave_fold,
     wave_last,
     wave_tail,
     wave_piece,
     recv,
+    recv_fold,
     recv_tail,
     back,
+    back_fold,
     back_tail,
     field,
+    field_fold,
     field_tail,
     field_piece,
-    relay,
     kernel_table,
     kernel_tail,
     total,
@@ -278,18 +281,14 @@
     visit_recv,
     give_send,
     give_recv,
-    wave_send,
-    wave_recv,
+    part_send,
+    part_recv,
+    fold_send,
+    fold_recv,
     tail_send,
     tail_recv,
-    back_send,
-    back_recv,
     back_tail_send,
     back_tail_recv,
-    copy_sem,
-    hop_send,
-    hop_recv,
-    forward_send,
     load_sem,
 ):
     me = lax.axis_index("pencil")
@@ -414,7 +413,7 @@
     wave_tail[...] = jnp.zeros((2, ROWS, 128), jnp.float32)
     for s in range(2):
         for p in range(PEERS):
-            back[s, (p + 1) * BLOCK - 8 : (p + 1) * BLOCK, :] = jnp.zeros((8, 128), jnp.float32)
+            back_fold[s, (p + 1) * LAST - 8 : (p + 1) * LAST, :] = jnp.zeros((8, 128), jnp.float32)
             back_tail[s, (p + 1) * PIECE - 8 : (p + 1) * PIECE, :] = jnp.zeros((8, 128), jnp.float32)
         field_tail[s, 32:40, :] = jnp.zeros((8, 128), jnp.float32)
         for f in range(FIELDS):
@@ -450,7 +449,7 @@
     def place(part, b, t):
         return pl.ds(pl.multiple_of((part * 9 + b) * ROWS + t * 8, 8), 8)
 
-    def first(s, between):
+    def first(s):
         arriving = visit_copies(s, (own, own_fold), visit_send.at[0], group_at(1))
         arriving[4].wait_recv()
         relays = lower_relays()
@@ -486,7 +485,6 @@
                 base = (part * 9 + b) * ROWS
                 work[base : base + ROWS, :] = parts[part]
         along_z(0)
-        between()
 
         def finish(t, target):
             def load(part, b):
@@ -496,19 +494,6 @@
                 put(target, slot * NG, value)
 
             finish72(load, save)
-
-        def planes(t, carry):
-            def target(tile, lanes, piece):
-                if tile == TAIL_TILE:
-                    wave_tail[s, pl.ds(pl.multiple_of(t * 8, 8), 8), lanes] = piece
-                else:
-                    start = tile // OWN_TILES * BLOCK + tile % OWN_TILES * 32
-                    wave[s, pl.ds(pl.multiple_of(start + t * 8, 8), 8), lanes] = piece
-
-            finish(t, target)
-            return carry
-
-        lax.fori_loop(0, 4, planes, 0)
 
         def last(tile, lanes, piece):
             if tile == TAIL_TILE:
@@ -517,9 +502,6 @@
                 wave_last[tile * 8 : tile * 8 + 8, lanes] = piece
 
         finish(4, last)
-        for f in range(FIELDS):
-            wave_piece[s, f, 0:8, :] = wave_tail[s, field_rows[f], :]
-            wave_piece[s, f, 8:9, :] = wave_tail[s, 32 + f : 33 + f, :]
         upper = lax.broadcasted_iota(jnp.int32, (8, 128), 0) < FIELDS
         for q in range(PEERS):
             for i in range(3):
@@ -527,79 +509,70 @@
                 piece = wave_last[tile : tile + 8, :]
                 if i < 2:
                     piece = jnp.where(upper, piece, wave_last[tile + 24 : tile + 32, :])
-                start = q * BLOCK + LAST + i * 8
-                wave[s, start : start + 8, :] = piece
-
-    def block_of(ref, s, index):
-        return ref.at[s, pl.ds(pl.multiple_of(index * BLOCK, 8), BLOCK), :]
-
-    def tail_of(ref, s, index):
-        return ref.at[s, pl.ds(pl.multiple_of(index * ROWS, 8), ROWS), :]
-
-    way = jnp.where(even, 1, -1)
-    exchange_refs = ((wave, recv, wave_send, wave_recv), (back, field, back_send, back_recv))
-
-    def hop(phase, s, dx):
-        return remote(
-            block_of(exchange_refs[phase][0], s, at(dx, 2)),
-            relay.at[phase, s, dx],
-            hop_send.at[phase, s, dx],
-            hop_recv.at[phase, s, dx],
-            pencil=at(dx, way),
-        )
-
-    def forward(phase, s, dx):
-        return remote(
-            relay.at[phase, s, dx],
-            block_of(exchange_refs[phase][1], s, at(dx, -way)),
-            forward_send.at[phase, s, dx],
-            exchange_refs[phase][3].at[s, dx * 4 + 2],
-            pencil=at(0, way),
-        )
-
-    def direct(phase, s, dx, dy):
-        src, dst, send, recv_sem = exchange_refs[phase]
-        return remote(
-            block_of(src, s, at(dx, dy)),
-            block_of(dst, s, me),
-            send.at[s, dx * 4 + dy],
-            recv_sem.at[s, dx * 4 + dy],
-            pencil=at(dx, dy),
-        )
-
-    straight = [(1, 1), (1, 3), (0, 1), (0, 3), (1, 0)]
-
-    def keep(phase, s):
-        src, dst = exchange_refs[phase][:2]
-        return pltpu.make_async_copy(
-            block_of(src, s, me), block_of(dst, s, me), copy_sem.at[phase, s]
-        )
-
-    def send_blocks(phase, s):
-        for dx in range(2):
-            hop(phase, s, dx).start()
+                wave_fold[s, q * LAST + i * 8 : q * LAST + i * 8 + 8, :] = piece
+        send_fold(0, s)
+
+        def planes(t, carry):
+            def target(tile, lanes, piece):
+                if tile == TAIL_TILE:
+                    wave_tail[s, pl.ds(pl.multiple_of(t * 8, 8), 8), lanes] = piece
+                else:
+                    wave[s, t, tile * 8 : tile * 8 + 8, lanes] = piece
+
+            finish(t, target)
+            send_part(0, s, t)
+            return carry
+
+        lax.fori_loop(0, FIELDS, planes, 0)
+        for f in range(FIELDS):
+            wave_piece[s, f, 0:8, :] = wave_tail[s, field_rows[f], :]
+            wave_piece[s, f, 8:9, :] = wave_tail[s, 32 + f : 33 + f, :]
+
+    part_refs = ((wave, recv), (back, field))
+    fold_refs = ((wave_fold, recv_fold), (back_fold, field_fold))
+    straight = [(1, 2), (0, 2), (1, 1), (1, 3), (0, 1), (0, 3), (1, 0)]
+
+    def rows_of(index, rows):
+        return pl.ds(pl.multiple_of(index * rows, 8), rows)
+
+    def send_part(phase, s, f):
+        src, dst = part_refs[phase]
         for dx, dy in straight:
-            direct(phase, s, dx, dy).start()
-        keep(phase, s).start()
-
-    def forward_blocks(phase, s):
-        for dx in range(2):
-            hop(phase, s, dx).wait_recv()
-            forward(phase, s, dx).start()
-
-    def wait_blocks(phase, s):
-        keep(phase, s).wait()
+            to = at(dx, dy)
+            remote(
+                src.at[s, f, rows_of(to, PART)],
+                dst.at[s, f, rows_of(me, PART)],
+                part_send.at[phase, s],
+                part_recv.at[phase, s, f],
+                pencil=to,
+            ).start()
+        dst[s, f, rows_of(me, PART), :] = src[s, f, rows_of(me, PART), :]
+
+    def send_fold(phase, s):
+        src, dst = fold_refs[phase]
         for dx, dy in straight:
-            direct(phase, s, dx, dy).wait_recv()
-        for dx in range(2):
-            forward(phase, s, dx).wait_recv()
+            to = at(dx, dy)
+            remote(
+                src.at[s, rows_of(to, LAST)],
+                dst.at[s, rows_of(me, LAST)],
+                fold_send.at[phase, s],
+                fold_recv.at[phase, s],
+                pencil=to,
+            ).start()
+        dst[s, rows_of(me, LAST), :] = src[s, rows_of(me, LAST), :]
+
+    def drain(view, sem):
+        pltpu.make_async_copy(view, view, sem).wait()
+
+    def wait_part(phase, s, f):
+        drain(part_refs[phase][1].at[s, f, pl.ds(0, 7 * PART)], part_recv.at[phase, s, f])
+
+    def wait_fold(phase, s):
+        drain(fold_refs[phase][1].at[s, pl.ds(0, 7 * LAST)], fold_recv.at[phase, s])
 
     def end_blocks(phase, s):
-        for dx, dy in straight:
-            direct(phase, s, dx, dy).wait_send()
-        for dx in range(2):
-            hop(phase, s, dx).wait_send()
-            forward(phase, s, dx).wait_send()
+        drain(part_refs[phase][0].at[s, :, pl.ds(0, 7 * PART)], part_send.at[phase, s])
+        drain(fold_refs[phase][0].at[s, pl.ds(0, 7 * LAST)], fold_send.at[phase, s])
 
     def piece_of(ref, s, index):
         return ref.at[s, pl.ds(pl.multiple_of(index * PIECE, 8), PIECE), :]
@@ -616,30 +589,30 @@
             pencil=jnp.int32(owner_of(s, f)),
         )
 
-    def lines(f, tile, block, last):
-        first_rows = [pl.ds(p * block + tile * 32 + f * 8, 8) for p in range(PEERS)]
-        below = FIELDS * (tile // 3)
-        return first_rows + [pl.ds(last + tile % 3 * 8 + below + f, PEERS, stride=block)]
-
-    def spectrum_step(source, target, s, tiles, table, block, last, fields):
-        columns = slice(tiles[0] * 128, (tiles[-1] + 1) * 128)
-        for f in fields:
-            rows = [lines(f, tile, block, last) for tile in tiles]
-            loaded = [
-                jnp.concatenate([source[s, part, :] for part in parts], axis=0) for parts in rows
-            ]
-            spectrum = left(wide[512:592, :], jnp.concatenate(loaded, axis=1))
-            result = left(wide[592:672, :], spectrum * table[:, columns])
-            for i, parts in enumerate(rows):
-                for j, part in enumerate(parts):
-                    target[s, part, :] = result[j * 8 : j * 8 + 8, i * 128 : (i + 1) * 128]
-
-    def second(s, between):
-        for half in range(2):
-            fields = range(2 * half, 2 * half + 2)
-            spectrum_step(recv, back, s, range(OWN_TILES), kernel_table, BLOCK, LAST, fields)
-            if half == 0:
-                between()
+    def second(s):
+        wait_fold(0, s)
+
+        def last_rows(f, tile):
+            return pl.ds(tile % 3 * 8 + FIELDS * (tile // 3) + f, PEERS, stride=LAST)
+
+        for f in range(FIELDS):
+            wait_part(0, s, f)
+            columns = []
+            for tile in range(OWN_TILES):
+                starts = [p * PART + tile * 8 for p in range(PEERS)]
+                rows = [recv[s, f, start : start + 8, :] for start in starts]
+                rows.append(recv_fold[s, last_rows(f, tile), :])
+                columns.append(jnp.concatenate(rows, axis=0))
+            spectrum = left(wide[512:592, :], jnp.concatenate(columns, axis=1))
+            result = left(wide[592:672, :], spectrum * kernel_table[...])
+            for tile in range(OWN_TILES):
+                lanes = slice(tile * 128, tile * 128 + 128)
+                for p in range(PEERS):
+                    start = p * PART + tile * 8
+                    back[s, f, start : start + 8, :] = result[p * 8 : p * 8 + 8, lanes]
+                back_fold[s, last_rows(f, tile), :] = result[64:72, lanes]
+            send_part(1, s, f)
+        send_fold(1, s)
 
     def give_copies(s):
         return block_copies(
@@ -659,7 +632,7 @@
             visitor_group[0],
         )
 
-    def third(s, between):
+    def third(s):
         def start(t, source):
             def load(slot):
                 return take(source, slot * NG)
@@ -670,28 +643,29 @@
             finish72_adjoint(load, save)
 
         def planes(t, carry):
+            wait_part(1, s, t)
+
             def source(tile):
                 if tile == TAIL_TILE:
                     return field_tail[s, pl.ds(pl.multiple_of(t * 8, 8), 8), :]
-                first_row = tile // OWN_TILES * BLOCK + tile % OWN_TILES * 32
-                return field[s, pl.ds(pl.multiple_of(first_row + t * 8, 8), 8), :]
+                return field[s, t, tile * 8 : tile * 8 + 8, :]
 
             start(t, source)
             return carry
 
-        lax.fori_loop(0, 4, planes, 0)
+        lax.fori_loop(0, FIELDS, planes, 0)
+        wait_fold(1, s)
 
         def last(tile):
             if tile == TAIL_TILE:
                 return field_tail[s, 32:40, :]
             which = tile % OWN_TILES
-            first_row = tile // OWN_TILES * BLOCK + LAST + which % 3 * 8
-            value = field[s, first_row : first_row + 8, :]
+            first_row = tile // OWN_TILES * LAST + which % 3 * 8
+            value = field_fold[s, first_row : first_row + 8, :]
             return pltpu.roll(value, FIELDS, 0) if which > 2 else value
 
         start(4, last)
         along_z(256)
-        between()
         for b in range(9):
             parts = []
             for part in range(8):
@@ -813,36 +787,18 @@
             for j in range(1, PEERS):
                 tail_back(s, lax.rem(me, FIELDS), j).wait_send()
 
-    def nothing():
-        pass
-
-    def forwards(*which):
-        def run():
-            for phase, s in which:
-                forward_blocks(phase, s)
-
-        return run
-
-    first(0, nothing)
-    send_blocks(0, 0)
+    first(0)
     send_tail(0)
-    first(1, forwards((0, 0)))
-    send_blocks(0, 1)
+    first(1)
     send_tail(1)
-    wait_blocks(0, 0)
-    second(0, forwards((0, 1)))
-    send_blocks(1, 0)
+    second(0)
     turn_tail(0)
-    wait_blocks(0, 1)
-    second(1, forwards((1, 0)))
-    send_blocks(1, 1)
+    second(1)
     turn_tail(1)
-    wait_blocks(1, 0)
     end_tail(0)
-    third(0, forwards((1, 1)))
-    wait_blocks(1, 1)
+    third(0)
     end_tail(1)
-    third(1, nothing)
+    third(1)
     for q, (begin, end) in enumerate(QUARTERS):
         for source in range(2):
             given_copies(source)[q].wait_recv()
@@ -908,18 +864,21 @@
             buffer(TILES, ROWS, 128),
             buffer(NG * ROWS, 128),
             buffer(NG * ROWS, 128),
-            buffer(2, PEERS * BLOCK, 128),
+            buffer(2, FIELDS, PEERS * PART, 128),
+            buffer(2, PEERS * LAST, 128),
             buffer(TAIL_TILE * 8, 128),
             buffer(2, ROWS, 128),
             buffer(2, FIELDS, PIECE, 128),
-            buffer(2, PEERS * BLOCK, 128),
+            buffer(2, FIELDS, PEERS * PART, 128),
+            buffer(2, PEERS * LAST, 128),
             buffer(2, PEERS * PIECE, 128),
-            buffer(2, PEERS * BLOCK, 128),
+            buffer(2, FIELDS, PEERS * PART, 128),
+            buffer(2, PEERS * LAST, 128),
             buffer(2, PEERS * PIECE, 128),
-            buffer(2, PEERS * BLOCK, 128),
+            buffer(2, FIELDS, PEERS * PART, 128),
+            buffer(2, PEERS * LAST, 128),
             buffer(2, ROWS, 128),
             buffer(2, FIELDS, PIECE, 128),
-            buffer(2, 2, 2, BLOCK, 128),
             buffer(NG, OWN),
             buffer(NG, 128),
             buffer(TILES, 16, 128),
@@ -932,18 +891,14 @@
             dma((2, 5)),
             dma((2, 5)),
             dma((2, 5)),
+            dma((2, 2)),
+            dma((2, 2, FIELDS)),
+            dma((2, 2)),
+            dma((2, 2)),
+            dma((2, FIELDS)),
             dma((2, PEERS)),
             dma((2, PEERS)),
             dma((2, FIELDS)),
-            dma((2, PEERS)),
-            dma((2, PEERS)),
-            dma((2, PEERS)),
-            dma((2, PEERS)),
-            dma((2, FIELDS)),
-            dma((2, 2)),
-            dma((2, 2, 2)),
-            dma((2, 2, 2)),
-            dma((2, 2, 2)),
             dma((4,)),
         ],
         compiler_params=pltpu.CompilerParams(

time: 68.8 us -> 69.1 us (level)
  the two profiles are of different devices: /device:TPU:24 before, /device:TPU:193 now
where the time goes in v2:
time: 69.1 us; the launch traced here: 68.9 us
  Pallas kernels  67.2 us (97%)
  local copies, waits for them, and re-layouts  1.76 us (3%)
    pallas_call x1, Pallas kernels, body(): pl.pallas_call(functools.partial(kernel, bands), out_shape=jax.ShapeDtype...  67.2 us
    unnamed x1, local copies, waits for them, and re-layouts  1.76 us

profile of v2, /device:TPU:193, one launch (start us, length us, event | category | flops | bytes accessed | tf_op | source)
XLA Modules:
  0.0 68.9 jit_solution(16702640176481183605)
XLA Ops:
  0.0 67.2 %shard_map.55 = f32[9,2,5184]{2,1,0:T(2,128)} custom-call(s32[1,2,2,2]{3,2,1,0:T(2,128)} %mask_ref.1, f32[9,2,5184]{2,1,0:T(2,128)} %bitcast.3, bf16[672,256]{1,0:T(8,128)(2,1)} %constant.6.clone.wide_hbm, f32[8,5248]{1,0:T(8,128)} %constant.7.clone.column_hbm, f32[72,128]{1,0:T(8,128)} %constant.8.clone.freq_hbm), custom_call_target="tpu_custom_call" | custom-call | tf_op jit(solution)/shard_map/pallas_call | solution.py:849
  67.2 1.8 %copy.7 = f32[2,9,5184]{2,0,1:T(2,128)} copy(f32[2,9,5184]{2,0,1:T(2,128)} %bitcast.2) | data formatting | bytes 746496

commit v3 on v2

--- a/solution.py
+++ b/solution.py
@@ -256,7 +256,6 @@
     work2,
     wave,
     wave_fold,
-    wave_last,
     wave_tail,
     wave_piece,
     recv,
@@ -324,18 +323,29 @@
     for j in (-2, -1, 1, 2):
         pl.semaphore_signal(barrier, inc=1, device_id={"band": group_at(j)}, device_id_type=MESH)
     loads[0].wait()
-    for tile in range(TILES):
-        lanes = slice(tile * 128, min(tile * 128 + 128, MERGED))
-        live = slice(0, lanes.stop - lanes.start)
-        if tile == TAIL_TILE:
-            mixed[tile] = jnp.zeros((16, 128), jnp.float32)
-            own_fold[tile % FOLD, 6:8, :] = jnp.zeros((2, 128), jnp.float32)
+    def take_tile(tile, j, q, width):
+        lanes = pl.ds(tile * 128, width)
+        if width == 128:
+            lanes = pl.ds(pl.multiple_of(tile * 128, 128), 128)
+        live = slice(0, width)
         for plane in range(PLANES - 1):
             mixed[tile, 2 * plane : 2 * plane + 2, live] = bands_ref[plane, :, lanes]
         for band in range(2):
             own[tile, band * 8 : band * 8 + 8, :] = mixed[tile, pl.ds(band, 8, stride=2), :]
-        row = tile // FOLD * 2
-        own_fold[tile % FOLD, row : row + 2, live] = bands_ref[PLANES - 1, :, lanes]
+        own_fold[j, 2 * q : 2 * q + 2, live] = bands_ref[PLANES - 1, :, lanes]
+
+    def tile_loop(begin, end, step):
+        def run(j, carry):
+            step(begin + j, j)
+            return carry
+
+        lax.fori_loop(0, end - begin, run, 0)
+
+    mixed[TAIL_TILE] = jnp.zeros((16, 128), jnp.float32)
+    own_fold[TAIL_TILE % FOLD, 6:8, :] = jnp.zeros((2, 128), jnp.float32)
+    for q, (begin, end) in enumerate(QUARTERS):
+        tile_loop(begin, min(end, TAIL_TILE), lambda tile, j, q=q: take_tile(tile, j, q, 128))
+    take_tile(TAIL_TILE, TAIL_TILE % FOLD, 3, MERGED - TAIL)
 
     def own_mask(s, f):
         return mask_ref[0, s, f // 2, f % 2].astype(jnp.float32)
@@ -357,10 +367,10 @@
 
     odd = lax.rem(group, 2)
     even = odd == 0
-    visitor_group = (
-        jnp.where(even, group_at(2), group_at(1)),
-        jnp.where(even, group_at(1), group_at(-2)),
-    )
+
+    def visitor_group(s):
+        near = jnp.where(even, group_at(2), group_at(1))
+        return jnp.where(s == 0, near, jnp.where(even, group_at(1), group_at(-2)))
 
     def parts(main, fold):
         return [
@@ -411,6 +421,13 @@
     kernel_table[...] = kernel_columns(pl.multiple_of(me * OWN, 128), OWN)
     kernel_tail[...] = kernel_columns(TAIL, 128)
     wave_tail[...] = jnp.zeros((2, ROWS, 128), jnp.float32)
+    total_fold[...] = jnp.zeros((FOLD + 1, 8, 128), jnp.float32)
+
+    def clear(tile, carry):
+        total[tile] = jnp.zeros((16, 128), jnp.float32)
+        return carry
+
+    lax.fori_loop(0, TILES, clear, 0)
     for s in range(2):
         for p in range(PEERS):
             back_fold[s, (p + 1) * LAST - 8 : (p + 1) * LAST, :] = jnp.zeros((8, 128), jnp.float32)
@@ -436,94 +453,92 @@
         )
 
     def along_z(start):
-        table = wide[start : start + 256, :]
-
-        def step(i, carry):
-            rows = pl.ds(pl.multiple_of(i * 720, 720), 720)
-            both = matmul(jnp.concatenate(halves(work[rows, :]), axis=1), table)
+        for i in range(2):
+            rows = pl.ds(i * 288, 288)
+            both = matmul(jnp.concatenate(halves(work[rows, :]), axis=1), wide[start : start + 256, :])
             work2[rows, :] = both[:, :128] + both[:, 128:]
-            return carry
-
-        lax.fori_loop(0, NG * ROWS // 720, step, 0)
-
-    def place(part, b, t):
-        return pl.ds(pl.multiple_of((part * 9 + b) * ROWS + t * 8, 8), 8)
+
+    def place(part, b):
+        return slice((part * 9 + b) * 8, (part * 9 + b) * 8 + 8)
+
+    def row_of(t):
+        return pl.ds(pl.multiple_of(t * 8, 8), 8)
 
     def first(s):
         arriving = visit_copies(s, (own, own_fold), visit_send.at[0], group_at(1))
-        arriving[4].wait_recv()
         relays = lower_relays()
-        if s == 0:
-
-            @pl.when(even)
+        for q in (4, 0, 1, 2, 3):
+            arriving[q].wait_recv()
+
+            @pl.when((s == 0) & even)
+            def _(q=q):
+                relays[q].start()
+
+        def one_row(i, carry):
+            t = lax.rem(i + FIELDS, FIELDS + 1)
+
+            @pl.when(i > 0)
             def _():
-                relays[4].start()
-
-        for q, (begin, end) in enumerate(QUARTERS):
-            arriving[q].wait_recv()
-            if s == 0:
-
-                @pl.when(even)
-                def _(q=q):
-                    relays[q].start()
-
-            def products(j, carry, q=q, begin=begin):
-                tile = begin + j
-                phi = [own[tile, rows, :] for rows in first_band]
-                chi = [visit[s, tile, rows, :] for rows in first_band]
-                for f in range(FIELDS):
-                    rho[tile, field_rows[f], :] = phi[f // 2] * chi[f % 2]
-                phi, chi = last_planes(s, j, q)
-                rho[tile, 32:40, :] = phi * chi
-                return carry
-
-            lax.fori_loop(0, end - begin, products, 0, unroll=True)
-        for b in range(9):
-            starts = [point72(a, b) * NG for a in range(8)]
-            parts = dft8([take(lambda i: rho[i], at) for at in starts])
-            for part in range(8):
-                base = (part * 9 + b) * ROWS
-                work[base : base + ROWS, :] = parts[part]
-        along_z(0)
-
-        def finish(t, target):
+                resident, visitor = row_of(lax.div(t, 2)), row_of(lax.rem(t, 2))
+                for tile in range(TILES):
+                    rho[tile, row_of(t), :] = own[tile, resident, :] * visit[s, tile, visitor, :]
+
+            @pl.when(i == 0)
+            def _():
+                for q, (begin, end) in enumerate(QUARTERS):
+
+                    def products(tile, j, q=q):
+                        phi, chi = last_planes(s, j, q)
+                        rho[tile, 32:40, :] = phi * chi
+
+                    tile_loop(begin, end, products)
+
+            for b in range(9):
+                starts = [point72(a, b) * NG for a in range(8)]
+                values = [take(lambda tile: rho[tile, row_of(t), :], at) for at in starts]
+                for part, value in enumerate(dft8(values)):
+                    work[place(part, b), :] = value
+            along_z(0)
+
             def load(part, b):
-                return work2[place(part, b, t), :]
+                return work2[place(part, b), :]
+
+            def target(tile, lanes, piece):
+                if tile == TAIL_TILE:
+                    wave_tail[s, row_of(t), lanes] = piece
+                else:
+                    wave[s, t, tile * 8 : tile * 8 + 8, lanes] = piece
 
             def save(slot, value):
                 put(target, slot * NG, value)
 
             finish72(load, save)
 
-        def last(tile, lanes, piece):
-            if tile == TAIL_TILE:
-                wave_tail[s, 32:40, lanes] = piece
-            else:
-                wave_last[tile * 8 : tile * 8 + 8, lanes] = piece
-
-        finish(4, last)
-        upper = lax.broadcasted_iota(jnp.int32, (8, 128), 0) < FIELDS
-        for q in range(PEERS):
-            for i in range(3):
-                tile = (q * OWN_TILES + i) * 8
-                piece = wave_last[tile : tile + 8, :]
-                if i < 2:
-                    piece = jnp.where(upper, piece, wave_last[tile + 24 : tile + 32, :])
-                wave_fold[s, q * LAST + i * 8 : q * LAST + i * 8 + 8, :] = piece
-        send_fold(0, s)
-
-        def planes(t, carry):
-            def target(tile, lanes, piece):
-                if tile == TAIL_TILE:
-                    wave_tail[s, pl.ds(pl.multiple_of(t * 8, 8), 8), lanes] = piece
-                else:
-                    wave[s, t, tile * 8 : tile * 8 + 8, lanes] = piece
-
-            finish(t, target)
-            send_part(0, s, t)
+            @pl.when(i == 0)
+            def _():
+                upper = lax.broadcasted_iota(jnp.int32, (8, 128), 0) < FIELDS
+
+                def fold(q, carry):
+                    for k in range(3):
+                        at_row = pl.multiple_of((q * OWN_TILES + k) * 8, 8)
+                        piece = wave[s, FIELDS, pl.ds(at_row, 8), :]
+                        if k < 2:
+                            below = wave[s, FIELDS, pl.ds(at_row + 24, 8), :]
+                            piece = jnp.where(upper, piece, below)
+                        to_row = pl.multiple_of(q * LAST + k * 8, 8)
+                        wave_fold[s, pl.ds(to_row, 8), :] = piece
+                    return carry
+
+                lax.fori_loop(0, PEERS, fold, 0)
+                send_fold(0, s)
+
+            @pl.when(i > 0)
+            def _():
+                send_part(0, s, t)
+
             return carry
 
-        lax.fori_loop(0, FIELDS, planes, 0)
+        lax.fori_loop(0, FIELDS + 1, one_row, 0)
         for f in range(FIELDS):
             wave_piece[s, f, 0:8, :] = wave_tail[s, field_rows[f], :]
             wave_piece[s, f, 8:9, :] = wave_tail[s, 32 + f : 33 + f, :]
@@ -571,7 +586,8 @@
         drain(fold_refs[phase][1].at[s, pl.ds(0, 7 * LAST)], fold_recv.at[phase, s])
 
     def end_blocks(phase, s):
-        drain(part_refs[phase][0].at[s, :, pl.ds(0, 7 * PART)], part_send.at[phase, s])
+        parts = part_refs[phase][0].at[s, pl.ds(0, FIELDS), pl.ds(0, 7 * PART)]
+        drain(parts, part_send.at[phase, s])
         drain(fold_refs[phase][0].at[s, pl.ds(0, 7 * LAST)], fold_send.at[phase, s])
 
     def piece_of(ref, s, index):
@@ -586,7 +602,7 @@
             piece_of(recv_tail, s, me),
             tail_send.at[s, f],
             tail_recv.at[s, distance],
-            pencil=jnp.int32(owner_of(s, f)),
+            pencil=owner_of(s, f),
         )
 
     def second(s):
@@ -595,7 +611,7 @@
         def last_rows(f, tile):
             return pl.ds(tile % 3 * 8 + FIELDS * (tile // 3) + f, PEERS, stride=LAST)
 
-        for f in range(FIELDS):
+        def one_field(f, carry):
             wait_part(0, s, f)
             columns = []
             for tile in range(OWN_TILES):
@@ -612,6 +628,9 @@
                     back[s, f, start : start + 8, :] = result[p * 8 : p * 8 + 8, lanes]
                 back_fold[s, last_rows(f, tile), :] = result[64:72, lanes]
             send_part(1, s, f)
+            return carry
+
+        lax.fori_loop(0, FIELDS, one_field, 0)
         send_fold(1, s)
 
     def give_copies(s):
@@ -620,7 +639,7 @@
             (given.at[odd], given_fold.at[odd]),
             give_send.at[s],
             give_recv.at[odd],
-            visitor_group[s],
+            visitor_group(s),
         )
 
     def given_copies(source):
@@ -629,70 +648,61 @@
             (given.at[source], given_fold.at[source]),
             give_send.at[0],
             give_recv.at[source],
-            visitor_group[0],
+            visitor_group(0),
         )
 
     def third(s):
-        def start(t, source):
+        def one_row(t, carry):
+            @pl.when(t < FIELDS)
+            def _():
+                wait_part(1, s, t)
+
+            @pl.when(t == FIELDS)
+            def _():
+                wait_fold(1, s)
+
+                def unfold(q, carry):
+                    for k in range(OWN_TILES):
+                        from_row = pl.multiple_of(q * LAST + k % 3 * 8, 8)
+                        value = field_fold[s, pl.ds(from_row, 8), :]
+                        value = pltpu.roll(value, FIELDS, 0) if k > 2 else value
+                        to_row = pl.multiple_of((q * OWN_TILES + k) * 8, 8)
+                        field[s, FIELDS, pl.ds(to_row, 8), :] = value
+                    return carry
+
+                lax.fori_loop(0, PEERS, unfold, 0)
+
+            def source(tile):
+                if tile == TAIL_TILE:
+                    return field_tail[s, row_of(t), :]
+                return field[s, t, tile * 8 : tile * 8 + 8, :]
+
             def load(slot):
                 return take(source, slot * NG)
 
             def save(part, b, value):
-                work[place(part, b, t), :] = value
+                work[place(part, b), :] = value
 
             finish72_adjoint(load, save)
-
-        def planes(t, carry):
-            wait_part(1, s, t)
-
-            def source(tile):
-                if tile == TAIL_TILE:
-                    return field_tail[s, pl.ds(pl.multiple_of(t * 8, 8), 8), :]
-                return field[s, t, tile * 8 : tile * 8 + 8, :]
-
-            start(t, source)
+            along_z(256)
+
+            def target(tile, lanes, piece):
+                rho[tile, row_of(t), lanes] = piece
+
+            for b in range(9):
+                values = dft8_adjoint([work2[place(part, b), :] for part in range(8)])
+                for a, value in enumerate(values):
+                    put(target, point72(a, b) * NG, value)
             return carry
 
-        lax.fori_loop(0, FIELDS, planes, 0)
-        wait_fold(1, s)
-
-        def last(tile):
-            if tile == TAIL_TILE:
-                return field_tail[s, 32:40, :]
-            which = tile % OWN_TILES
-            first_row = tile // OWN_TILES * LAST + which % 3 * 8
-            value = field_fold[s, first_row : first_row + 8, :]
-            return pltpu.roll(value, FIELDS, 0) if which > 2 else value
-
-        start(4, last)
-        along_z(256)
-        for b in range(9):
-            parts = []
-            for part in range(8):
-                base = (part * 9 + b) * ROWS
-                parts.append(work2[base : base + ROWS, :])
-            for a, value in enumerate(dft8_adjoint(parts)):
-
-
-                def store(tile, lanes, piece):
-                    rho[tile, :, lanes] = piece
-
-                put(store, point72(a, b) * NG, value)
+        lax.fori_loop(0, FIELDS + 1, one_row, 0)
         weights = []
         for f in range(FIELDS):
             g = 2 * (f % 2) + f // 2
-            if s == 0:
-                row = jnp.where(
-                    even,
-                    visit_fold[s, MASKS, FIELDS + g : FIELDS + g + 1, :],
-                    visit_fold[s, MASKS, g : g + 1, :],
-                )
-            else:
-                row = jnp.where(
-                    even,
-                    visit_fold[s, MASKS, g : g + 1, :],
-                    own_fold[MASKS, FIELDS + f : FIELDS + f + 1, :],
-                )
+            above = visit_fold[s, MASKS, FIELDS + g : FIELDS + g + 1, :]
+            same = visit_fold[s, MASKS, g : g + 1, :]
+            mine = own_fold[MASKS, FIELDS + f : FIELDS + f + 1, :]
+            row = jnp.where(s == 0, jnp.where(even, above, same), jnp.where(even, same, mine))
             weights.append(jnp.broadcast_to(row, (8, 128)))
         last_weight = weights[3]
         for f in range(3):
@@ -701,16 +711,13 @@
         leaving = give_copies(s)
         for q, (begin, end) in enumerate(QUARTERS):
 
-            def gather(j, carry, q=q, begin=begin):
-                tile = begin + j
+            def gather(tile, j, q=q):
                 phi = [own[tile, rows, :] for rows in first_band]
                 chi = [visit[s, tile, rows, :] for rows in first_band]
                 value = [rho[tile, field_rows[f], :] * weights[f] for f in range(FIELDS)]
                 for a in range(2):
                     stay = value[2 * a] * chi[0] + value[2 * a + 1] * chi[1]
-                    if s > 0:
-                        stay = stay + total[tile, first_band[a], :]
-                    total[tile, first_band[a], :] = stay
+                    total[tile, first_band[a], :] += stay
                 for c in range(2):
                     give[s, tile, first_band[c], :] = value[c] * phi[0] + value[2 + c] * phi[1]
                 phi, chi = last_planes(s, j, q)
@@ -720,14 +727,10 @@
                 leave = leave + pltpu.roll(leave, 6, 0)
                 for band in range(2):
                     row = slice(2 * q + band, 2 * q + band + 1)
-                    kept = stay[2 * band : 2 * band + 1]
-                    if s > 0:
-                        kept = kept + total_fold[j, row, :]
-                    total_fold[j, row, :] = kept
+                    total_fold[j, row, :] += stay[2 * band : 2 * band + 1]
                     give_fold[s, j, row, :] = leave[band : band + 1]
-                return carry
-
-            lax.fori_loop(0, end - begin, gather, 0, unroll=True)
+
+            tile_loop(begin, end, gather)
             leaving[q].start()
         leaving[4].start()
 
@@ -746,7 +749,7 @@
 
             @pl.when(me == owner)
             def _(f=f, owner=owner):
-                recv_tail[s, owner * PIECE : (owner + 1) * PIECE, :] = wave_piece[s, f]
+                recv_tail[s, rows_of(owner, PIECE), :] = wave_piece[s, f]
 
             @pl.when(me != owner)
             def _(f=f, owner=owner):
@@ -787,37 +790,51 @@
             for j in range(1, PEERS):
                 tail_back(s, lax.rem(me, FIELDS), j).wait_send()
 
-    first(0)
-    send_tail(0)
-    first(1)
-    send_tail(1)
-    second(0)
-    turn_tail(0)
-    second(1)
-    turn_tail(1)
-    end_tail(0)
-    third(0)
-    end_tail(1)
-    third(1)
+    def slots(*stages):
+        def run(s, carry):
+            for stage in stages:
+                stage(s)
+            return carry
+
+        lax.fori_loop(0, 2, run, 0)
+
+    slots(first, send_tail)
+    slots(second, turn_tail)
+    slots(end_tail, third)
+
     for q, (begin, end) in enumerate(QUARTERS):
         for source in range(2):
             given_copies(source)[q].wait_recv()
-        for tile in range(begin, end):
-            lanes = slice(tile * 128, min(tile * 128 + 128, MERGED))
+
+        def result(tile, j, width=128):
+            lanes = pl.ds(tile * 128, width)
+            if width == 128:
+                lanes = pl.ds(pl.multiple_of(tile * 128, 128), 128)
             for rows, band in zip(first_band, range(2)):
                 term = -(total[tile, rows, :] + given[0, tile, rows, :] + given[1, tile, rows, :])
                 mixed[tile, pl.ds(band, 8, stride=2), :] = term
             for plane in range(PLANES - 1):
-                piece = mixed[tile, 2 * plane : 2 * plane + 2, 0 : lanes.stop - lanes.start]
+                piece = mixed[tile, 2 * plane : 2 * plane + 2, 0:width]
                 out_ref[plane, :, lanes] = piece
+
+        tile_loop(begin, min(end, TAIL_TILE), result)
+        if end > TAIL_TILE:
+            result(TAIL_TILE, 0, MERGED - TAIL)
     for source in range(2):
         given_copies(source)[4].wait_recv()
     for q, (begin, end) in enumerate(QUARTERS):
-        for tile in range(begin, end):
-            lanes = slice(tile * 128, min(tile * 128 + 128, MERGED))
-            j, rows = tile - begin, slice(2 * q, 2 * q + 2)
+
+        def last_result(tile, j, q=q, width=128):
+            lanes = pl.ds(tile * 128, width)
+            if width == 128:
+                lanes = pl.ds(pl.multiple_of(tile * 128, 128), 128)
+            rows = slice(2 * q, 2 * q + 2)
             term = total_fold[j, rows, :] + given_fold[0, j, rows, :] + given_fold[1, j, rows, :]
-            out_ref[PLANES - 1, :, lanes] = -term[:, 0 : lanes.stop - lanes.start]
+            out_ref[PLANES - 1, :, lanes] = -term[:, 0:width]
+
+        tile_loop(begin, min(end, TAIL_TILE), last_result)
+        if end > TAIL_TILE:
+            last_result(TAIL_TILE, TAIL_TILE - begin, width=MERGED - TAIL)
 
     @pl.when(even)
     def _():
@@ -862,11 +879,10 @@
             buffer(2, TILES, 16, 128),
             buffer(2, FOLD + 1, 8, 128),
             buffer(TILES, ROWS, 128),
-            buffer(NG * ROWS, 128),
-            buffer(NG * ROWS, 128),
-            buffer(2, FIELDS, PEERS * PART, 128),
+            buffer(NG * 8, 128),
+            buffer(NG * 8, 128),
+            buffer(2, FIELDS + 1, PEERS * PART, 128),
             buffer(2, PEERS * LAST, 128),
-            buffer(TAIL_TILE * 8, 128),
             buffer(2, ROWS, 128),
             buffer(2, FIELDS, PIECE, 128),
             buffer(2, FIELDS, PEERS * PART, 128),
@@ -875,7 +891,7 @@
             buffer(2, FIELDS, PEERS * PART, 128),
             buffer(2, PEERS * LAST, 128),
             buffer(2, PEERS * PIECE, 128),
-            buffer(2, FIELDS, PEERS * PART, 128),
+            buffer(2, FIELDS + 1, PEERS * PART, 128),
             buffer(2, PEERS * LAST, 128),
             buffer(2, ROWS, 128),
             buffer(2, FIELDS, PIECE, 128),

time: 69.1 us -> 68.3 us (0.988)
  Pallas kernels: 67.2 us -> 66.4 us
    pallas_call x1, Pallas kernels: 67.2 us -> 66.4 us  [body(): pl.pallas_call(functools.partial(kernel, bands), out_shape=jax.ShapeDtype...]
where the time goes in v3:
time: 68.3 us; the launch traced here: 68.2 us
  Pallas kernels  66.4 us (97%)
  local copies, waits for them, and re-layouts  1.76 us (3%)
    pallas_call x1, Pallas kernels, body(): pl.pallas_call(functools.partial(kernel, bands), out_shape=jax.ShapeDtype...  66.4 us
    unnamed x1, local copies, waits for them, and re-layouts  1.76 us

profile of v3, /device:TPU:193, one launch (start us, length us, event | category | flops | bytes accessed | tf_op | source)
XLA Modules:
  0.0 68.2 jit_solution(8795365357927826480)
XLA Ops:
  0.0 66.4 %shard_map.55 = f32[9,2,5184]{2,1,0:T(2,128)} custom-call(s32[1,2,2,2]{3,2,1,0:T(2,128)} %mask_ref.1, f32[9,2,5184]{2,1,0:T(2,128)} %bitcast.3, bf16[672,256]{1,0:T(8,128)(2,1)} %constant.6.clone.wide_hbm, f32[8,5248]{1,0:T(8,128)} %constant.7.clone.column_hbm, f32[72,128]{1,0:T(8,128)} %constant.8.clone.freq_hbm), custom_call_target="tpu_custom_call" | custom-call | tf_op jit(solution)/shard_map/pallas_call | solution.py:866
  66.4 1.8 %copy.7 = f32[2,9,5184]{2,0,1:T(2,128)} copy(f32[2,9,5184]{2,0,1:T(2,128)} %bitcast.2) | data formatting | bytes 746496

commit v4 on v3

--- a/solution.py
+++ b/solution.py
@@ -369,7 +369,7 @@
     even = odd == 0
 
     def visitor_group(s):
-        near = jnp.where(even, group_at(2), group_at(1))
+        near = jnp.where(even, group_at(2), group_at(-1))
         return jnp.where(s == 0, near, jnp.where(even, group_at(1), group_at(-2)))
 
     def parts(main, fold):
@@ -381,24 +381,29 @@
     def block_copies(src, dst, send, recv, to):
         return [
             remote(one, two, send.at[q], recv.at[q], band=to)
-            for q, (one, two) in enumerate(zip(parts(*src), parts(*dst)))
+            for q, (one, two) in enumerate(zip(src, dst))
         ]
 
     def visit_at(s):
-        return visit.at[s], visit_fold.at[s]
+        return parts(visit.at[s], visit_fold.at[s])
+
+    own_parts = parts(own, own_fold)
+
+    def give_parts(main, fold):
+        return [main.at[0], *parts(main.at[1], fold)]
 
     def visit_copies(s, src, send, to):
         return block_copies(src, visit_at(s), send, visit_recv.at[s], to)
 
     def lower_sends():
-        return visit_copies(0, (own, own_fold), visit_send.at[0], group_at(-2))
+        return visit_copies(0, own_parts, visit_send.at[0], group_at(-2))
 
     def lower_relays():
         return visit_copies(0, visit_at(0), visit_send.at[1], group_at(1))
 
     def upper_sends():
-        return visit_copies(1, (own, own_fold), visit_send.at[0], group_at(2)) + visit_copies(
-            1, (own, own_fold), visit_send.at[1], group_at(-1)
+        return visit_copies(1, own_parts, visit_send.at[0], group_at(2)) + visit_copies(
+            1, own_parts, visit_send.at[1], group_at(-1)
         )
 
     @pl.when(even)
@@ -465,7 +470,7 @@
         return pl.ds(pl.multiple_of(t * 8, 8), 8)
 
     def first(s):
-        arriving = visit_copies(s, (own, own_fold), visit_send.at[0], group_at(1))
+        arriving = visit_copies(s, own_parts, visit_send.at[0], group_at(1))
         relays = lower_relays()
         for q in (4, 0, 1, 2, 3):
             arriving[q].wait_recv()
@@ -475,7 +480,7 @@
                 relays[q].start()
 
         def one_row(i, carry):
-            t = lax.rem(i + FIELDS, FIELDS + 1)
+            t = jnp.where(i == 0, FIELDS, order(jnp.maximum(i - 1, 0)))
 
             @pl.when(i > 0)
             def _():
@@ -611,7 +616,8 @@
         def last_rows(f, tile):
             return pl.ds(tile % 3 * 8 + FIELDS * (tile // 3) + f, PEERS, stride=LAST)
 
-        def one_field(f, carry):
+        def one_field(i, carry):
+            f = order(i)
             wait_part(0, s, f)
             columns = []
             for tile in range(OWN_TILES):
@@ -635,8 +641,8 @@
 
     def give_copies(s):
         return block_copies(
-            (give.at[s], give_fold.at[s]),
-            (given.at[odd], given_fold.at[odd]),
+            give_parts(give.at[s], give_fold.at[s]),
+            give_parts(given.at[odd], given_fold.at[odd]),
             give_send.at[s],
             give_recv.at[odd],
             visitor_group(s),
@@ -644,15 +650,73 @@
 
     def given_copies(source):
         return block_copies(
-            (give.at[0], give_fold.at[0]),
-            (given.at[source], given_fold.at[source]),
+            give_parts(give.at[0], give_fold.at[0]),
+            give_parts(given.at[source], given_fold.at[source]),
             give_send.at[0],
             give_recv.at[source],
             visitor_group(0),
         )
 
+    def join():
+        for copy in given_copies(1):
+            copy.wait_recv()
+
+        def add(tile, carry):
+            for band in range(2):
+                give[0, band, tile] += given[1, band, tile]
+                given[1, band, tile] = jnp.zeros((8, 128), jnp.float32)
+            return carry
+
+        lax.fori_loop(0, TILES, add, 0)
+        give_fold[0] = give_fold[0] + given_fold[1]
+        given_fold[1] = jnp.zeros((FOLD + 1, 8, 128), jnp.float32)
+        for copy in give_copies(0):
+            copy.start()
+
+    def order(i):
+        return lax.rem(2 * i, FIELDS) + lax.div(i, 2)
+
+    def pair_weights(s):
+        weights = []
+        for f in range(FIELDS):
+            g = 2 * (f % 2) + f // 2
+            above = visit_fold[s, MASKS, FIELDS + g : FIELDS + g + 1, :]
+            same = visit_fold[s, MASKS, g : g + 1, :]
+            mine = own_fold[MASKS, FIELDS + f : FIELDS + f + 1, :]
+            row = jnp.where(s == 0, jnp.where(even, above, same), jnp.where(even, same, mine))
+            weights.append(jnp.broadcast_to(row, (8, 128)))
+        return weights
+
     def third(s):
-        def one_row(t, carry):
+        weights = pair_weights(s)
+        leaving = give_copies(s)
+        held = (s == 0) & even
+
+        def leave(which):
+            @pl.when(jnp.logical_not(held))
+            def _():
+                for part in which:
+                    leaving[part].start()
+
+        def gather_band(c, begin, end):
+            def gather(tile, j):
+                chi = visit[s, tile, first_band[c], :]
+                terms = jnp.zeros((8, 128), jnp.float32)
+                for a in range(2):
+                    value = rho[tile, field_rows[2 * a + c], :] * weights[2 * a + c]
+                    total[tile, first_band[a], :] += value * chi
+                    terms = terms + value * own[tile, first_band[a], :]
+                give[s, c, tile] = terms
+
+            tile_loop(begin, end, gather)
+
+        def one_row(i, carry):
+            t = jnp.where(i == FIELDS, FIELDS, order(jnp.minimum(i, FIELDS - 1)))
+
+            @pl.when((s == 1) & even & (i == 2))
+            def _():
+                join()
+
             @pl.when(t < FIELDS)
             def _():
                 wait_part(1, s, t)
@@ -693,33 +757,24 @@
                 values = dft8_adjoint([work2[place(part, b), :] for part in range(8)])
                 for a, value in enumerate(values):
                     put(target, point72(a, b) * NG, value)
+
+            @pl.when(i == 1)
+            def _():
+                gather_band(0, 0, TILES)
+                leave([0])
+
             return carry
 
         lax.fori_loop(0, FIELDS + 1, one_row, 0)
-        weights = []
-        for f in range(FIELDS):
-            g = 2 * (f % 2) + f // 2
-            above = visit_fold[s, MASKS, FIELDS + g : FIELDS + g + 1, :]
-            same = visit_fold[s, MASKS, g : g + 1, :]
-            mine = own_fold[MASKS, FIELDS + f : FIELDS + f + 1, :]
-            row = jnp.where(s == 0, jnp.where(even, above, same), jnp.where(even, same, mine))
-            weights.append(jnp.broadcast_to(row, (8, 128)))
         last_weight = weights[3]
         for f in range(3):
             last_weight = jnp.where(row_at == f, weights[f], last_weight)
 
-        leaving = give_copies(s)
         for q, (begin, end) in enumerate(QUARTERS):
-
-            def gather(tile, j, q=q):
-                phi = [own[tile, rows, :] for rows in first_band]
-                chi = [visit[s, tile, rows, :] for rows in first_band]
-                value = [rho[tile, field_rows[f], :] * weights[f] for f in range(FIELDS)]
-                for a in range(2):
-                    stay = value[2 * a] * chi[0] + value[2 * a + 1] * chi[1]
-                    total[tile, first_band[a], :] += stay
-                for c in range(2):
-                    give[s, tile, first_band[c], :] = value[c] * phi[0] + value[2 + c] * phi[1]
+            gather_band(1, begin, end)
+            leave([1 + q])
+
+            def gather_last(tile, j, q=q):
                 phi, chi = last_planes(s, j, q)
                 value = rho[tile, 32:40, :] * last_weight
                 stay, leave = value * chi, value * phi
@@ -730,9 +785,8 @@
                     total_fold[j, row, :] += stay[2 * band : 2 * band + 1]
                     give_fold[s, j, row, :] = leave[band : band + 1]
 
-            tile_loop(begin, end, gather)
-            leaving[q].start()
-        leaving[4].start()
+            tile_loop(begin, end, gather_last)
+        leave([5])
 
     def tail_back(s, f, j):
         return remote(
@@ -802,16 +856,23 @@
     slots(second, turn_tail)
     slots(end_tail, third)
 
+    def wait_given(which):
+        for part in which:
+            given_copies(0)[part].wait_recv()
+
+            @pl.when(jnp.logical_not(even))
+            def _(part=part):
+                given_copies(1)[part].wait_recv()
+
     for q, (begin, end) in enumerate(QUARTERS):
-        for source in range(2):
-            given_copies(source)[q].wait_recv()
+        wait_given([0, 1] if q == 0 else [1 + q])
 
         def result(tile, j, width=128):
             lanes = pl.ds(tile * 128, width)
             if width == 128:
                 lanes = pl.ds(pl.multiple_of(tile * 128, 128), 128)
             for rows, band in zip(first_band, range(2)):
-                term = -(total[tile, rows, :] + given[0, tile, rows, :] + given[1, tile, rows, :])
+                term = -(total[tile, rows, :] + given[0, band, tile] + given[1, band, tile])
                 mixed[tile, pl.ds(band, 8, stride=2), :] = term
             for plane in range(PLANES - 1):
                 piece = mixed[tile, 2 * plane : 2 * plane + 2, 0:width]
@@ -820,8 +881,7 @@
         tile_loop(begin, min(end, TAIL_TILE), result)
         if end > TAIL_TILE:
             result(TAIL_TILE, 0, MERGED - TAIL)
-    for source in range(2):
-        given_copies(source)[4].wait_recv()
+    wait_given([5])
     for q, (begin, end) in enumerate(QUARTERS):
 
         def last_result(tile, j, q=q, width=128):
@@ -899,14 +959,14 @@
             buffer(NG, 128),
             buffer(TILES, 16, 128),
             buffer(FOLD + 1, 8, 128),
-            buffer(2, TILES, 16, 128),
+            buffer(2, 2, TILES, 8, 128),
             buffer(2, FOLD + 1, 8, 128),
-            buffer(2, TILES, 16, 128),
+            buffer(2, 2, TILES, 8, 128),
             buffer(2, FOLD + 1, 8, 128),
             dma((2, 5)),
             dma((2, 5)),
-            dma((2, 5)),
-            dma((2, 5)),
+            dma((2, 6)),
+            dma((2, 6)),
             dma((2, 2)),
             dma((2, 2, FIELDS)),
             dma((2, 2)),

time: 68.3 us -> 72.9 us (1.067)
  the two profiles are of different devices: /device:TPU:193 before, /device:TPU:24 now
where the time goes in v4:
time: 72.9 us; the launch traced here: 72.4 us
  Pallas kernels  70.6 us (97%)
  local copies, waits for them, and re-layouts  1.76 us (2%)
    pallas_call x1, Pallas kernels, body(): pl.pallas_call(functools.partial(kernel, bands), out_shape=jax.ShapeDtype...  70.6 us
    unnamed x1, local copies, waits for them, and re-layouts  1.76 us

profile of v4, /device:TPU:24, one launch (start us, length us, event | category | flops | bytes accessed | tf_op | source)
XLA Modules:
  0.0 72.4 jit_solution(2009621773051310805)
XLA Ops:
  0.0 70.6 %shard_map.55 = f32[9,2,5184]{2,1,0:T(2,128)} custom-call(s32[1,2,2,2]{3,2,1,0:T(2,128)} %mask_ref.1, f32[9,2,5184]{2,1,0:T(2,128)} %bitcast.3, bf16[672,256]{1,0:T(8,128)(2,1)} %constant.6.clone.wide_hbm, f32[8,5248]{1,0:T(8,128)} %constant.7.clone.column_hbm, f32[72,128]{1,0:T(8,128)} %constant.8.clone.freq_hbm), custom_call_target="tpu_custom_call" | custom-call | tf_op jit(solution)/shard_map/pallas_call | solution.py:926
  70.6 1.8 %copy.7 = f32[2,9,5184]{2,0,1:T(2,128)} copy(f32[2,9,5184]{2,0,1:T(2,128)} %bitcast.2) | data formatting | bytes 746496

commit v5 on v4

--- a/solution.py
+++ b/solution.py
@@ -272,6 +272,8 @@
     kernel_tail,
     total,
     total_fold,
+    base,
+    base_fold,
     give,
     give_fold,
     given,
@@ -365,12 +367,11 @@
             device_id_type=MESH,
         )
 
-    odd = lax.rem(group, 2)
-    even = odd == 0
-
-    def visitor_group(s):
-        near = jnp.where(even, group_at(2), group_at(-1))
-        return jnp.where(s == 0, near, jnp.where(even, group_at(1), group_at(-2)))
+    even = lax.rem(group, 2) == 0
+
+    def terms_group(s):
+        near = jnp.where(even, group_at(1), group_at(-1))
+        return jnp.where(s == 0, near, jnp.where(even, group_at(2), group_at(-2)))
 
     def parts(main, fold):
         return [
@@ -395,25 +396,19 @@
     def visit_copies(s, src, send, to):
         return block_copies(src, visit_at(s), send, visit_recv.at[s], to)
 
-    def lower_sends():
-        return visit_copies(0, own_parts, visit_send.at[0], group_at(-2))
-
-    def lower_relays():
-        return visit_copies(0, visit_at(0), visit_send.at[1], group_at(1))
-
-    def upper_sends():
-        return visit_copies(1, own_parts, visit_send.at[0], group_at(2)) + visit_copies(
-            1, own_parts, visit_send.at[1], group_at(-1)
-        )
-
-    @pl.when(even)
-    def _():
-        for copy in lower_sends():
-            copy.start()
+    def near_sends():
+        return visit_copies(0, own_parts, visit_send.at[0], group_at(-1))
+
+    def far_sends():
+        to = jnp.where(even, group_at(-2), group_at(2))
+        return visit_copies(1, own_parts, visit_send.at[1], to)
+
+    for copy in near_sends():
+        copy.start()
 
     @pl.when(jnp.logical_not(even))
     def _():
-        for copy in upper_sends():
+        for copy in far_sends():
             copy.start()
 
     def kernel_columns(start, width):
@@ -427,9 +422,11 @@
     kernel_tail[...] = kernel_columns(TAIL, 128)
     wave_tail[...] = jnp.zeros((2, ROWS, 128), jnp.float32)
     total_fold[...] = jnp.zeros((FOLD + 1, 8, 128), jnp.float32)
+    base_fold[...] = jnp.zeros((FOLD + 1, 8, 128), jnp.float32)
 
     def clear(tile, carry):
         total[tile] = jnp.zeros((16, 128), jnp.float32)
+        base[:, tile] = jnp.zeros((2, 8, 128), jnp.float32)
         return carry
 
     lax.fori_loop(0, TILES, clear, 0)
@@ -471,16 +468,16 @@
 
     def first(s):
         arriving = visit_copies(s, own_parts, visit_send.at[0], group_at(1))
-        relays = lower_relays()
         for q in (4, 0, 1, 2, 3):
             arriving[q].wait_recv()
 
-            @pl.when((s == 0) & even)
-            def _(q=q):
-                relays[q].start()
-
         def one_row(i, carry):
             t = jnp.where(i == 0, FIELDS, order(jnp.maximum(i - 1, 0)))
+
+            @pl.when((s == 0) & even & (i == 2))
+            def _():
+                for copy in far_sends():
+                    copy.start()
 
             @pl.when(i > 0)
             def _():
@@ -642,36 +639,11 @@
     def give_copies(s):
         return block_copies(
             give_parts(give.at[s], give_fold.at[s]),
-            give_parts(given.at[odd], given_fold.at[odd]),
+            give_parts(given.at[s], given_fold.at[s]),
             give_send.at[s],
-            give_recv.at[odd],
-            visitor_group(s),
+            give_recv.at[s],
+            terms_group(s),
         )
-
-    def given_copies(source):
-        return block_copies(
-            give_parts(give.at[0], give_fold.at[0]),
-            give_parts(given.at[source], given_fold.at[source]),
-            give_send.at[0],
-            give_recv.at[source],
-            visitor_group(0),
-        )
-
-    def join():
-        for copy in given_copies(1):
-            copy.wait_recv()
-
-        def add(tile, carry):
-            for band in range(2):
-                give[0, band, tile] += given[1, band, tile]
-                given[1, band, tile] = jnp.zeros((8, 128), jnp.float32)
-            return carry
-
-        lax.fori_loop(0, TILES, add, 0)
-        give_fold[0] = give_fold[0] + given_fold[1]
-        given_fold[1] = jnp.zeros((FOLD + 1, 8, 128), jnp.float32)
-        for copy in give_copies(0):
-            copy.start()
 
     def order(i):
         return lax.rem(2 * i, FIELDS) + lax.div(i, 2)
@@ -683,25 +655,22 @@
             above = visit_fold[s, MASKS, FIELDS + g : FIELDS + g + 1, :]
             same = visit_fold[s, MASKS, g : g + 1, :]
             mine = own_fold[MASKS, FIELDS + f : FIELDS + f + 1, :]
-            row = jnp.where(s == 0, jnp.where(even, above, same), jnp.where(even, same, mine))
+            row = jnp.where(s == 0, same, jnp.where(even, above, mine))
             weights.append(jnp.broadcast_to(row, (8, 128)))
         return weights
 
     def third(s):
         weights = pair_weights(s)
         leaving = give_copies(s)
-        held = (s == 0) & even
 
         def leave(which):
-            @pl.when(jnp.logical_not(held))
-            def _():
-                for part in which:
-                    leaving[part].start()
+            for part in which:
+                leaving[part].start()
 
         def gather_band(c, begin, end):
             def gather(tile, j):
                 chi = visit[s, tile, first_band[c], :]
-                terms = jnp.zeros((8, 128), jnp.float32)
+                terms = base[c, tile]
                 for a in range(2):
                     value = rho[tile, field_rows[2 * a + c], :] * weights[2 * a + c]
                     total[tile, first_band[a], :] += value * chi
@@ -712,10 +681,6 @@
 
         def one_row(i, carry):
             t = jnp.where(i == FIELDS, FIELDS, order(jnp.minimum(i, FIELDS - 1)))
-
-            @pl.when((s == 1) & even & (i == 2))
-            def _():
-                join()
 
             @pl.when(t < FIELDS)
             def _():
@@ -757,6 +722,19 @@
                 values = dft8_adjoint([work2[place(part, b), :] for part in range(8)])
                 for a, value in enumerate(values):
                     put(target, point72(a, b) * NG, value)
+
+            @pl.when((s == 1) & even & (i == 1))
+            def _():
+                for copy in give_copies(0):
+                    copy.wait_recv()
+
+                def join(tile, carry):
+                    for band in range(2):
+                        base[band, tile] = given[0, band, tile]
+                    return carry
+
+                lax.fori_loop(0, TILES, join, 0)
+                base_fold[...] = given_fold[0]
 
             @pl.when(i == 1)
             def _():
@@ -783,7 +761,7 @@
                 for band in range(2):
                     row = slice(2 * q + band, 2 * q + band + 1)
                     total_fold[j, row, :] += stay[2 * band : 2 * band + 1]
-                    give_fold[s, j, row, :] = leave[band : band + 1]
+                    give_fold[s, j, row, :] = leave[band : band + 1] + base_fold[j, row, :]
 
             tile_loop(begin, end, gather_last)
         leave([5])
@@ -858,11 +836,11 @@
 
     def wait_given(which):
         for part in which:
-            given_copies(0)[part].wait_recv()
+            give_copies(1)[part].wait_recv()
 
             @pl.when(jnp.logical_not(even))
             def _(part=part):
-                given_copies(1)[part].wait_recv()
+                give_copies(0)[part].wait_recv()
 
     for q, (begin, end) in enumerate(QUARTERS):
         wait_given([0, 1] if q == 0 else [1 + q])
@@ -872,7 +850,8 @@
             if width == 128:
                 lanes = pl.ds(pl.multiple_of(tile * 128, 128), 128)
             for rows, band in zip(first_band, range(2)):
-                term = -(total[tile, rows, :] + given[0, band, tile] + given[1, band, tile])
+                near = jnp.where(even, 0.0, given[0, band, tile])
+                term = -(total[tile, rows, :] + near + given[1, band, tile])
                 mixed[tile, pl.ds(band, 8, stride=2), :] = term
             for plane in range(PLANES - 1):
                 piece = mixed[tile, 2 * plane : 2 * plane + 2, 0:width]
@@ -889,22 +868,16 @@
             if width == 128:
                 lanes = pl.ds(pl.multiple_of(tile * 128, 128), 128)
             rows = slice(2 * q, 2 * q + 2)
-            term = total_fold[j, rows, :] + given_fold[0, j, rows, :] + given_fold[1, j, rows, :]
+            near = jnp.where(even, 0.0, given_fold[0, j, rows, :])
+            term = total_fold[j, rows, :] + near + given_fold[1, j, rows, :]
             out_ref[PLANES - 1, :, lanes] = -term[:, 0:width]
 
         tile_loop(begin, min(end, TAIL_TILE), last_result)
         if end > TAIL_TILE:
             last_result(TAIL_TILE, TAIL_TILE - begin, width=MERGED - TAIL)
 
-    @pl.when(even)
-    def _():
-        for copy in lower_sends() + lower_relays():
-            copy.wait_send()
-
-    @pl.when(jnp.logical_not(even))
-    def _():
-        for copy in upper_sends():
-            copy.wait_send()
+    for copy in near_sends() + far_sends():
+        copy.wait_send()
 
     for s in range(2):
         for copy in give_copies(s):
@@ -959,6 +932,8 @@
             buffer(NG, 128),
             buffer(TILES, 16, 128),
             buffer(FOLD + 1, 8, 128),
+            buffer(2, TILES, 8, 128),
+            buffer(FOLD + 1, 8, 128),
             buffer(2, 2, TILES, 8, 128),
             buffer(2, FOLD + 1, 8, 128),
             buffer(2, 2, TILES, 8, 128),

time: 72.9 us -> 73.3 us (level)
  Pallas kernels: 70.6 us -> 71.4 us
    pallas_call x1, Pallas kernels: 70.6 us -> 71.4 us  [body(): pl.pallas_call(functools.partial(kernel, bands), out_shape=jax.ShapeDtype...]
where the time goes in v5:
time: 73.3 us; the launch traced here: 73.2 us
  Pallas kernels  71.4 us (97%)
  local copies, waits for them, and re-layouts  1.76 us (2%)
    pallas_call x1, Pallas kernels, body(): pl.pallas_call(functools.partial(kernel, bands), out_shape=jax.ShapeDtype...  71.4 us
    unnamed x1, local copies, waits for them, and re-layouts  1.76 us

profile of v5, /device:TPU:24, one launch (start us, length us, event | category | flops | bytes accessed | tf_op | source)
XLA Modules:
  0.0 73.2 jit_solution(12581044722193442984)
XLA Ops:
  0.0 71.4 %shard_map.55 = f32[9,2,5184]{2,1,0:T(2,128)} custom-call(s32[1,2,2,2]{3,2,1,0:T(2,128)} %mask_ref.1, f32[9,2,5184]{2,1,0:T(2,128)} %bitcast.3, bf16[672,256]{1,0:T(8,128)(2,1)} %constant.6.clone.wide_hbm, f32[8,5248]{1,0:T(8,128)} %constant.7.clone.column_hbm, f32[72,128]{1,0:T(8,128)} %constant.8.clone.freq_hbm), custom_call_target="tpu_custom_call" | custom-call | tf_op jit(solution)/shard_map/pallas_call | solution.py:899
  71.4 1.8 %copy.7 = f32[2,9,5184]{2,0,1:T(2,128)} copy(f32[2,9,5184]{2,0,1:T(2,128)} %bitcast.2) | data formatting | bytes 746496

commit v6 on v5

--- a/solution.py
+++ b/solution.py
@@ -280,6 +280,7 @@
     given_fold,
     visit_send,
     visit_recv,
+    pass_send,
     give_send,
     give_recv,
     part_send,
@@ -400,8 +401,10 @@
         return visit_copies(0, own_parts, visit_send.at[0], group_at(-1))
 
     def far_sends():
-        to = jnp.where(even, group_at(-2), group_at(2))
-        return visit_copies(1, own_parts, visit_send.at[1], to)
+        return visit_copies(1, own_parts, visit_send.at[1], group_at(2))
+
+    def passes():
+        return visit_copies(1, visit_at(0), pass_send, group_at(-1))
 
     for copy in near_sends():
         copy.start()
@@ -468,16 +471,16 @@
 
     def first(s):
         arriving = visit_copies(s, own_parts, visit_send.at[0], group_at(1))
+        passing = passes()
         for q in (4, 0, 1, 2, 3):
             arriving[q].wait_recv()
 
+            @pl.when((s == 0) & jnp.logical_not(even))
+            def _(q=q):
+                passing[q].start()
+
         def one_row(i, carry):
             t = jnp.where(i == 0, FIELDS, order(jnp.maximum(i - 1, 0)))
-
-            @pl.when((s == 0) & even & (i == 2))
-            def _():
-                for copy in far_sends():
-                    copy.start()
 
             @pl.when(i > 0)
             def _():
@@ -876,8 +879,13 @@
         if end > TAIL_TILE:
             last_result(TAIL_TILE, TAIL_TILE - begin, width=MERGED - TAIL)
 
-    for copy in near_sends() + far_sends():
+    for copy in near_sends():
         copy.wait_send()
+
+    @pl.when(jnp.logical_not(even))
+    def _():
+        for copy in far_sends() + passes():
+            copy.wait_send()
 
     for s in range(2):
         for copy in give_copies(s):
@@ -940,6 +948,7 @@
             buffer(2, FOLD + 1, 8, 128),
             dma((2, 5)),
             dma((2, 5)),
+            dma((5,)),
             dma((2, 6)),
             dma((2, 6)),
             dma((2, 2)),

time: 73.3 us -> 63.2 us (0.86); the launches traced: 73.2 us -> 62 us
  Pallas kernels: 71.4 us -> 60.2 us
    pallas_call x1, Pallas kernels: 71.4 us -> 60.2 us  [body(): pl.pallas_call(functools.partial(kernel, bands), out_shape=jax.ShapeDtype...]
where the time goes in v6:
time: 63.2 us; the launch traced here: 62 us
  Pallas kernels  60.2 us (95%)
  local copies, waits for them, and re-layouts  1.76 us (3%)
    pallas_call x1, Pallas kernels, body(): pl.pallas_call(functools.partial(kernel, bands), out_shape=jax.ShapeDtype...  60.2 us
    unnamed x1, local copies, waits for them, and re-layouts  1.76 us

profile of v6, /device:TPU:24, one launch (start us, length us, event | category | flops | bytes accessed | tf_op | source)
XLA Modules:
  0.0 62.0 jit_solution(7567276359271961295)
XLA Ops:
  0.0 60.2 %shard_map.55 = f32[9,2,5184]{2,1,0:T(2,128)} custom-call(s32[1,2,2,2]{3,2,1,0:T(2,128)} %mask_ref.1, f32[9,2,5184]{2,1,0:T(2,128)} %bitcast.3, bf16[672,256]{1,0:T(8,128)(2,1)} %constant.6.clone.wide_hbm, f32[8,5248]{1,0:T(8,128)} %constant.7.clone.column_hbm, f32[72,128]{1,0:T(8,128)} %constant.8.clone.freq_hbm), custom_call_target="tpu_custom_call" | custom-call | tf_op jit(solution)/shard_map/pallas_call | solution.py:907
  60.2 1.8 %copy.7 = f32[2,9,5184]{2,0,1:T(2,128)} copy(f32[2,9,5184]{2,0,1:T(2,128)} %bitcast.2) | data formatting | bytes 746496

commit v7 on v6

--- a/solution.py
+++ b/solution.py
@@ -325,6 +325,54 @@
         pl.semaphore_signal(barrier, inc=1, device_id={"pencil": peer(j)}, device_id_type=MESH)
     for j in (-2, -1, 1, 2):
         pl.semaphore_signal(barrier, inc=1, device_id={"band": group_at(j)}, device_id_type=MESH)
+    def remote(src, dst, send, recv, **device):
+        return pltpu.make_async_remote_copy(
+            src_ref=src,
+            dst_ref=dst,
+            send_sem=send,
+            recv_sem=recv,
+            device_id=device,
+            device_id_type=MESH,
+        )
+
+    even = lax.rem(group, 2) == 0
+
+    def terms_group(s):
+        near = jnp.where(even, group_at(1), group_at(-1))
+        return jnp.where(s == 0, near, jnp.where(even, group_at(2), group_at(-2)))
+
+    def parts(main, fold):
+        return [
+            *(main.at[pl.ds(begin, end - begin)] for begin, end in QUARTERS),
+            fold,
+        ]
+
+    def block_copies(src, dst, send, recv, to):
+        return [
+            remote(one, two, send.at[q], recv.at[q], band=to)
+            for q, (one, two) in enumerate(zip(src, dst))
+        ]
+
+    def visit_at(s):
+        return parts(visit.at[s], visit_fold.at[s])
+
+    own_parts = parts(own, own_fold)
+
+    def give_parts(main, fold):
+        return [main.at[0], *parts(main.at[1], fold)]
+
+    def visit_copies(s, src, send, to):
+        return block_copies(src, visit_at(s), send, visit_recv.at[s], to)
+
+    def near_sends():
+        return visit_copies(0, own_parts, visit_send.at[0], group_at(-1))
+
+    def far_sends():
+        return visit_copies(1, own_parts, visit_send.at[1], group_at(2))
+
+    def passes():
+        return visit_copies(1, visit_at(0), pass_send, group_at(-1))
+
     loads[0].wait()
     def take_tile(tile, j, q, width):
         lanes = pl.ds(tile * 128, width)
@@ -342,13 +390,10 @@
             step(begin + j, j)
             return carry
 
-        lax.fori_loop(0, end - begin, run, 0)
+        lax.fori_loop(0, end - begin, run, 0, unroll=True)
 
     mixed[TAIL_TILE] = jnp.zeros((16, 128), jnp.float32)
     own_fold[TAIL_TILE % FOLD, 6:8, :] = jnp.zeros((2, 128), jnp.float32)
-    for q, (begin, end) in enumerate(QUARTERS):
-        tile_loop(begin, min(end, TAIL_TILE), lambda tile, j, q=q: take_tile(tile, j, q, 128))
-    take_tile(TAIL_TILE, TAIL_TILE % FOLD, 3, MERGED - TAIL)
 
     def own_mask(s, f):
         return mask_ref[0, s, f // 2, f % 2].astype(jnp.float32)
@@ -357,62 +402,21 @@
         value = own_mask(m // FIELDS, m % FIELDS)
         own_fold[MASKS, m : m + 1, :] = jnp.zeros((1, 128), jnp.float32) + value
     pl.semaphore_wait(barrier, PEERS - 1 + 4)
-
-    def remote(src, dst, send, recv, **device):
-        return pltpu.make_async_remote_copy(
-            src_ref=src,
-            dst_ref=dst,
-            send_sem=send,
-            recv_sem=recv,
-            device_id=device,
-            device_id_type=MESH,
-        )
-
-    even = lax.rem(group, 2) == 0
-
-    def terms_group(s):
-        near = jnp.where(even, group_at(1), group_at(-1))
-        return jnp.where(s == 0, near, jnp.where(even, group_at(2), group_at(-2)))
-
-    def parts(main, fold):
-        return [
-            *(main.at[pl.ds(begin, end - begin)] for begin, end in QUARTERS),
-            fold,
-        ]
-
-    def block_copies(src, dst, send, recv, to):
-        return [
-            remote(one, two, send.at[q], recv.at[q], band=to)
-            for q, (one, two) in enumerate(zip(src, dst))
-        ]
-
-    def visit_at(s):
-        return parts(visit.at[s], visit_fold.at[s])
-
-    own_parts = parts(own, own_fold)
-
-    def give_parts(main, fold):
-        return [main.at[0], *parts(main.at[1], fold)]
-
-    def visit_copies(s, src, send, to):
-        return block_copies(src, visit_at(s), send, visit_recv.at[s], to)
-
-    def near_sends():
-        return visit_copies(0, own_parts, visit_send.at[0], group_at(-1))
-
-    def far_sends():
-        return visit_copies(1, own_parts, visit_send.at[1], group_at(2))
-
-    def passes():
-        return visit_copies(1, visit_at(0), pass_send, group_at(-1))
-
-    for copy in near_sends():
-        copy.start()
-
-    @pl.when(jnp.logical_not(even))
-    def _():
-        for copy in far_sends():
-            copy.start()
+    near, far = near_sends(), far_sends()
+
+    def send_own(part):
+        near[part].start()
+
+        @pl.when(jnp.logical_not(even))
+        def _():
+            far[part].start()
+
+    for q, (begin, end) in enumerate(QUARTERS):
+        tile_loop(begin, min(end, TAIL_TILE), lambda tile, j, q=q: take_tile(tile, j, q, 128))
+        if end > TAIL_TILE:
+            take_tile(TAIL_TILE, TAIL_TILE % FOLD, q, MERGED - TAIL)
+        send_own(q)
+    send_own(4)
 
     def kernel_columns(start, width):
         squared = column_ref[0:1, pl.ds(start, width)]
@@ -472,7 +476,7 @@
     def first(s):
         arriving = visit_copies(s, own_parts, visit_send.at[0], group_at(1))
         passing = passes()
-        for q in (4, 0, 1, 2, 3):
+        for q in range(5):
             arriving[q].wait_recv()
 
             @pl.when((s == 0) & jnp.logical_not(even))

time: 63.2 us -> 62.1 us (0.983)
  Pallas kernels: 60.2 us -> 59.4 us
    pallas_call x1, Pallas kernels: 60.2 us -> 59.4 us  [body(): pl.pallas_call(functools.partial(kernel, bands), out_shape=jax.ShapeDtype...]
where the time goes in v7:
time: 62.1 us; the launch traced here: 61.1 us
  Pallas kernels  59.4 us (96%)
  local copies, waits for them, and re-layouts  1.76 us (3%)
    pallas_call x1, Pallas kernels, body(): pl.pallas_call(functools.partial(kernel, bands), out_shape=jax.ShapeDtype...  59.4 us
    unnamed x1, local copies, waits for them, and re-layouts  1.76 us

profile of v7, /device:TPU:24, one launch (start us, length us, event | category | flops | bytes accessed | tf_op | source)
XLA Modules:
  0.0 61.1 jit_solution(5070885374545529349)
XLA Ops:
  0.0 59.4 %shard_map.55 = f32[9,2,5184]{2,1,0:T(2,128)} custom-call(s32[1,2,2,2]{3,2,1,0:T(2,128)} %mask_ref.1, f32[9,2,5184]{2,1,0:T(2,128)} %bitcast.3, bf16[672,256]{1,0:T(8,128)(2,1)} %constant.6.clone.wide_hbm, f32[8,5248]{1,0:T(8,128)} %constant.7.clone.column_hbm, f32[72,128]{1,0:T(8,128)} %constant.8.clone.freq_hbm), custom_call_target="tpu_custom_call" | custom-call | tf_op jit(solution)/shard_map/pallas_call | solution.py:911
  59.4 1.8 %copy.7 = f32[2,9,5184]{2,0,1:T(2,128)} copy(f32[2,9,5184]{2,0,1:T(2,128)} %bitcast.2) | data formatting | bytes 746496

commit v8 on v7

--- a/solution.py
+++ b/solution.py
@@ -462,10 +462,8 @@
         )
 
     def along_z(start):
-        for i in range(2):
-            rows = pl.ds(i * 288, 288)
-            both = matmul(jnp.concatenate(halves(work[rows, :]), axis=1), wide[start : start + 256, :])
-            work2[rows, :] = both[:, :128] + both[:, 128:]
+        both = matmul(jnp.concatenate(halves(work[...]), axis=1), wide[start : start + 256, :])
+        work2[...] = both[:, :128] + both[:, 128:]
 
     def place(part, b):
         return slice((part * 9 + b) * 8, (part * 9 + b) * 8 + 8)

time: 62.1 us -> 62.1 us (level)
  no operation moved by 1% of the time
where the time goes in v8:
time: 62.1 us; the launch traced here: 61.1 us
  Pallas kernels  59.4 us (96%)
  local copies, waits for them, and re-layouts  1.76 us (3%)
    pallas_call x1, Pallas kernels, body(): pl.pallas_call(functools.partial(kernel, bands), out_shape=jax.ShapeDtype...  59.4 us
    unnamed x1, local copies, waits for them, and re-layouts  1.76 us

profile of v8, /device:TPU:24, one launch (start us, length us, event | category | flops | bytes accessed | tf_op | source)
XLA Modules:
  0.0 61.1 jit_solution(4023507834387858006)
XLA Ops:
  0.0 59.4 %shard_map.55 = f32[9,2,5184]{2,1,0:T(2,128)} custom-call(s32[1,2,2,2]{3,2,1,0:T(2,128)} %mask_ref.1, f32[9,2,5184]{2,1,0:T(2,128)} %bitcast.3, bf16[672,256]{1,0:T(8,128)(2,1)} %constant.6.clone.wide_hbm, f32[8,5248]{1,0:T(8,128)} %constant.7.clone.column_hbm, f32[72,128]{1,0:T(8,128)} %constant.8.clone.freq_hbm), custom_call_target="tpu_custom_call" | custom-call | tf_op jit(solution)/shard_map/pallas_call | solution.py:909
  59.4 1.8 %copy.7 = f32[2,9,5184]{2,0,1:T(2,128)} copy(f32[2,9,5184]{2,0,1:T(2,128)} %bitcast.2) | data formatting | bytes 746496

commit v9 on v8

--- a/solution.py
+++ b/solution.py
@@ -746,6 +746,12 @@
                 gather_band(0, 0, TILES)
                 leave([0])
 
+            @pl.when(i == 3)
+            def _():
+                for q, (begin, end) in enumerate(QUARTERS):
+                    gather_band(1, begin, end)
+                    leave([1 + q])
+
             return carry
 
         lax.fori_loop(0, FIELDS + 1, one_row, 0)
@@ -754,8 +760,6 @@
             last_weight = jnp.where(row_at == f, weights[f], last_weight)
 
         for q, (begin, end) in enumerate(QUARTERS):
-            gather_band(1, begin, end)
-            leave([1 + q])
 
             def gather_last(tile, j, q=q):
                 phi, chi = last_planes(s, j, q)

time: 62.1 us -> 62.1 us (level)
  no operation moved by 1% of the time
where the time goes in v9:
time: 62.1 us; the launch traced here: 61.1 us
  Pallas kernels  59.4 us (96%)
  local copies, waits for them, and re-layouts  1.76 us (3%)
    pallas_call x1, Pallas kernels, body(): pl.pallas_call(functools.partial(kernel, bands), out_shape=jax.ShapeDtype...  59.4 us
    unnamed x1, local copies, waits for them, and re-layouts  1.76 us

profile of v9, /device:TPU:24, one launch (start us, length us, event | category | flops | bytes accessed | tf_op | source)
XLA Modules:
  0.0 61.1 jit_solution(14849410406871814557)
XLA Ops:
  0.0 59.4 %shard_map.55 = f32[9,2,5184]{2,1,0:T(2,128)} custom-call(s32[1,2,2,2]{3,2,1,0:T(2,128)} %mask_ref.1, f32[9,2,5184]{2,1,0:T(2,128)} %bitcast.3, bf16[672,256]{1,0:T(8,128)(2,1)} %constant.6.clone.wide_hbm, f32[8,5248]{1,0:T(8,128)} %constant.7.clone.column_hbm, f32[72,128]{1,0:T(8,128)} %constant.8.clone.freq_hbm), custom_call_target="tpu_custom_call" | custom-call | tf_op jit(solution)/shard_map/pallas_call | solution.py:913
  59.4 1.8 %copy.7 = f32[2,9,5184]{2,0,1:T(2,128)} copy(f32[2,9,5184]{2,0,1:T(2,128)} %bitcast.2) | data formatting | bytes 746496

commit v10 on v9

--- a/solution.py
+++ b/solution.py
@@ -353,10 +353,14 @@
             for q, (one, two) in enumerate(zip(src, dst))
         ]
 
+    def block_parts(main, fold):
+        first = [main.at[pl.ds(begin, end - begin), pl.ds(0, 8)] for begin, end in QUARTERS]
+        return [*first, fold, main.at[:, pl.ds(8, 8)]]
+
     def visit_at(s):
-        return parts(visit.at[s], visit_fold.at[s])
-
-    own_parts = parts(own, own_fold)
+        return block_parts(visit.at[s], visit_fold.at[s])
+
+    own_parts = block_parts(own, own_fold)
 
     def give_parts(main, fold):
         return [main.at[0], *parts(main.at[1], fold)]
@@ -417,6 +421,7 @@
             take_tile(TAIL_TILE, TAIL_TILE % FOLD, q, MERGED - TAIL)
         send_own(q)
     send_own(4)
+    send_own(5)
 
     def kernel_columns(start, width):
         squared = column_ref[0:1, pl.ds(start, width)]
@@ -474,15 +479,23 @@
     def first(s):
         arriving = visit_copies(s, own_parts, visit_send.at[0], group_at(1))
         passing = passes()
-        for q in range(5):
-            arriving[q].wait_recv()
+
+        def arrive(part):
+            arriving[part].wait_recv()
 
             @pl.when((s == 0) & jnp.logical_not(even))
-            def _(q=q):
-                passing[q].start()
+            def _():
+                passing[part].start()
+
+        for part in range(5):
+            arrive(part)
 
         def one_row(i, carry):
             t = jnp.where(i == 0, FIELDS, order(jnp.maximum(i - 1, 0)))
+
+            @pl.when(i == 3)
+            def _():
+                arrive(5)
 
             @pl.when(i > 0)
             def _():
@@ -952,9 +965,9 @@
             buffer(2, FOLD + 1, 8, 128),
             buffer(2, 2, TILES, 8, 128),
             buffer(2, FOLD + 1, 8, 128),
-            dma((2, 5)),
-            dma((2, 5)),
-            dma((5,)),
+            dma((2, 6)),
+            dma((2, 6)),
+            dma((6,)),
             dma((2, 6)),
             dma((2, 6)),
             dma((2, 2)),

time: 62.1 us -> 63.1 us (1.016); the launches traced: 61.1 us -> 62.9 us
  Pallas kernels: 59.4 us -> 61.2 us
    pallas_call x1, Pallas kernels: 59.4 us -> 61.2 us  [body(): pl.pallas_call(functools.partial(kernel, bands), out_shape=jax.ShapeDtype...]
where the time goes in v10:
time: 63.1 us; the launch traced here: 62.9 us
  Pallas kernels  61.2 us (97%)
  local copies, waits for them, and re-layouts  1.76 us (3%)
    pallas_call x1, Pallas kernels, body(): pl.pallas_call(functools.partial(kernel, bands), out_shape=jax.ShapeDtype...  61.2 us
    unnamed x1, local copies, waits for them, and re-layouts  1.76 us

profile of v10, /device:TPU:24, one launch (start us, length us, event | category | flops | bytes accessed | tf_op | source)
XLA Modules:
  0.0 62.9 jit_solution(13071216342146193550)
XLA Ops:
  0.0 61.2 %shard_map.55 = f32[9,2,5184]{2,1,0:T(2,128)} custom-call(s32[1,2,2,2]{3,2,1,0:T(2,128)} %mask_ref.1, f32[9,2,5184]{2,1,0:T(2,128)} %bitcast.3, bf16[672,256]{1,0:T(8,128)(2,1)} %constant.6.clone.wide_hbm, f32[8,5248]{1,0:T(8,128)} %constant.7.clone.column_hbm, f32[72,128]{1,0:T(8,128)} %constant.8.clone.freq_hbm), custom_call_target="tpu_custom_call" | custom-call | tf_op jit(solution)/shard_map/pallas_call | solution.py:926
  61.2 1.8 %copy.7 = f32[2,9,5184]{2,0,1:T(2,128)} copy(f32[2,9,5184]{2,0,1:T(2,128)} %bitcast.2) | data formatting | bytes 746496

commit v11 on v10

--- a/solution.py
+++ b/solution.py
@@ -741,26 +741,22 @@
                 for a, value in enumerate(values):
                     put(target, point72(a, b) * NG, value)
 
-            @pl.when((s == 1) & even & (i == 1))
-            def _():
-                for copy in give_copies(0):
-                    copy.wait_recv()
-
-                def join(tile, carry):
-                    for band in range(2):
-                        base[band, tile] = given[0, band, tile]
-                    return carry
-
-                lax.fori_loop(0, TILES, join, 0)
-                base_fold[...] = given_fold[0]
+            def join(band, which):
+                @pl.when((s == 1) & even)
+                def _():
+                    for part in which:
+                        give_copies(0)[part].wait_recv()
+                    base[band] = given[0, band]
 
             @pl.when(i == 1)
             def _():
+                join(0, [0])
                 gather_band(0, 0, TILES)
                 leave([0])
 
             @pl.when(i == 3)
             def _():
+                join(1, [1, 2, 3, 4])
                 for q, (begin, end) in enumerate(QUARTERS):
                     gather_band(1, begin, end)
                     leave([1 + q])
@@ -768,6 +764,12 @@
             return carry
 
         lax.fori_loop(0, FIELDS + 1, one_row, 0)
+
+        @pl.when((s == 1) & even)
+        def _():
+            give_copies(0)[5].wait_recv()
+            base_fold[...] = given_fold[0]
+
         last_weight = weights[3]
         for f in range(3):
             last_weight = jnp.where(row_at == f, weights[f], last_weight)

time: 63.1 us -> 62.9 us (level)
  no operation moved by 1% of the time
where the time goes in v11:
time: 62.9 us; the launch traced here: 62.7 us
  Pallas kernels  60.9 us (97%)
  local copies, waits for them, and re-layouts  1.76 us (3%)
    pallas_call x1, Pallas kernels, body(): pl.pallas_call(functools.partial(kernel, bands), out_shape=jax.ShapeDtype...  60.9 us
    unnamed x1, local copies, waits for them, and re-layouts  1.76 us

profile of v11, /device:TPU:24, one launch (start us, length us, event | category | flops | bytes accessed | tf_op | source)
XLA Modules:
  0.0 62.7 jit_solution(5796471241312243744)
XLA Ops:
  0.0 60.9 %shard_map.55 = f32[9,2,5184]{2,1,0:T(2,128)} custom-call(s32[1,2,2,2]{3,2,1,0:T(2,128)} %mask_ref.1, f32[9,2,5184]{2,1,0:T(2,128)} %bitcast.3, bf16[672,256]{1,0:T(8,128)(2,1)} %constant.6.clone.wide_hbm, f32[8,5248]{1,0:T(8,128)} %constant.7.clone.column_hbm, f32[72,128]{1,0:T(8,128)} %constant.8.clone.freq_hbm), custom_call_target="tpu_custom_call" | custom-call | tf_op jit(solution)/shard_map/pallas_call | solution.py:928
  61.0 1.8 %copy.7 = f32[2,9,5184]{2,0,1:T(2,128)} copy(f32[2,9,5184]{2,0,1:T(2,128)} %bitcast.2) | data formatting | bytes 746496

commit v12 on v9

--- a/solution.py
+++ b/solution.py
@@ -728,26 +728,22 @@
                 for a, value in enumerate(values):
                     put(target, point72(a, b) * NG, value)
 
-            @pl.when((s == 1) & even & (i == 1))
-            def _():
-                for copy in give_copies(0):
-                    copy.wait_recv()
-
-                def join(tile, carry):
-                    for band in range(2):
-                        base[band, tile] = given[0, band, tile]
-                    return carry
-
-                lax.fori_loop(0, TILES, join, 0)
-                base_fold[...] = given_fold[0]
+            def join(band, which):
+                @pl.when((s == 1) & even)
+                def _():
+                    for part in which:
+                        give_copies(0)[part].wait_recv()
+                    base[band] = given[0, band]
 
             @pl.when(i == 1)
             def _():
+                join(0, [0])
                 gather_band(0, 0, TILES)
                 leave([0])
 
             @pl.when(i == 3)
             def _():
+                join(1, [1, 2, 3, 4])
                 for q, (begin, end) in enumerate(QUARTERS):
                     gather_band(1, begin, end)
                     leave([1 + q])
@@ -755,6 +751,12 @@
             return carry
 
         lax.fori_loop(0, FIELDS + 1, one_row, 0)
+
+        @pl.when((s == 1) & even)
+        def _():
+            give_copies(0)[5].wait_recv()
+            base_fold[...] = given_fold[0]
+
         last_weight = weights[3]
         for f in range(3):
             last_weight = jnp.where(row_at == f, weights[f], last_weight)

time: 62.1 us -> 61.9 us (level)
  no operation moved by 1% of the time
where the time goes in v12:
time: 61.9 us; the launch traced here: 60.9 us
  Pallas kernels  59.1 us (95%)
  local copies, waits for them, and re-layouts  1.76 us (3%)
    pallas_call x1, Pallas kernels, body(): pl.pallas_call(functools.partial(kernel, bands), out_shape=jax.ShapeDtype...  59.1 us
    unnamed x1, local copies, waits for them, and re-layouts  1.76 us

profile of v12, /device:TPU:24, one launch (start us, length us, event | category | flops | bytes accessed | tf_op | source)
XLA Modules:
  0.0 60.9 jit_solution(5684186546203453383)
XLA Ops:
  0.0 59.1 %shard_map.55 = f32[9,2,5184]{2,1,0:T(2,128)} custom-call(s32[1,2,2,2]{3,2,1,0:T(2,128)} %mask_ref.1, f32[9,2,5184]{2,1,0:T(2,128)} %bitcast.3, bf16[672,256]{1,0:T(8,128)(2,1)} %constant.6.clone.wide_hbm, f32[8,5248]{1,0:T(8,128)} %constant.7.clone.column_hbm, f32[72,128]{1,0:T(8,128)} %constant.8.clone.freq_hbm), custom_call_target="tpu_custom_call" | custom-call | tf_op jit(solution)/shard_map/pallas_call | solution.py:915
  59.1 1.8 %copy.7 = f32[2,9,5184]{2,0,1:T(2,128)} copy(f32[2,9,5184]{2,0,1:T(2,128)} %bitcast.2) | data formatting | bytes 746496
